TPU v7x, 128 devices: a whole 4x4x4 slice. The times are simulated.
128 devices in a mesh: fsdp: 32 (over z, y_lo, x), tp: 4 (over y_hi, core).
Axes of the slice: x: 4, y: 4 (y_hi: 2, y_lo: 2; y = y_hi * 2 + y_lo), z: 4, core: 2. Of those that a mesh axis runs over, the one named last changes fastest.
Arguments:
- acts: bfloat16 [4096, 4096], P('fsdp', 'tp'), may hold values from -6 to 6
- gate_codes: int32 [14336, 4096], P('fsdp', 'tp'), may hold values from -8 to 7
- gate_scales: float32 [14336, 32], P('fsdp', 'tp'), may hold values from 0.0015 to 0.006
- up_codes: int32 [14336, 4096], P('fsdp', 'tp'), may hold values from -8 to 7
- up_scales: float32 [14336, 32], P('fsdp', 'tp'), may hold values from 0.0015 to 0.006
- down_codes: int32 [14336, 4096], P('fsdp', 'tp'), may hold values from -8 to 7
- down_scales: float32 [14336, 32], P('fsdp', 'tp'), may hold values from 0.0009 to 0.0036
- cotangent: bfloat16 [4096, 4096], P('fsdp', 'tp'), may hold values from -0.099609375 to 0.099609375
Outputs:
- output: bfloat16 [4096, 4096], P('fsdp', 'tp')
- grad_gate: float32 [14336, 4096], P('fsdp', 'tp')
- grad_up: float32 [14336, 4096], P('fsdp', 'tp')
- grad_down: float32 [14336, 4096], P('fsdp', 'tp')
All inputs are finite; a program needn't handle non-finite values.
Results may differ from a plain program's by a relative error of at most 0.035.
Values may be sent and summed in bfloat16 or wider, within the bound.
A program may use at most 128 MiB of HBM per device.

v0:
```python
import jax
import jax.numpy as jnp
from jax import lax
from jax.sharding import PartitionSpec as P

GROUP = 128


def dequantize(code_values, scale_values):
    num_rows, num_cols = code_values.shape
    grouped = (
        code_values.astype(jnp.float32).reshape(num_rows, num_cols // GROUP, GROUP)
        * scale_values[:, :, None]
    )
    return grouped.reshape(num_rows, num_cols).astype(jnp.bfloat16)


def contract_last(left_side, right_side):
    return lax.dot_general(
        left_side, right_side, (((1,), (1,)), ((), ())), preferred_element_type=jnp.float32
    )


def contract_first(left_side, right_side):
    return lax.dot_general(
        left_side, right_side, (((0,), (0,)), ((), ())), preferred_element_type=jnp.float32
    )


def silu_slope(values):
    logistic = jax.nn.sigmoid(values)
    return logistic * (1.0 + values * (1.0 - logistic))


def local_grads(grad_hidden, gate, up):
    grad_gate_act = (grad_hidden * up * silu_slope(gate)).astype(jnp.bfloat16)
    grad_up_act = (grad_hidden * jax.nn.silu(gate)).astype(jnp.bfloat16)
    return (grad_gate_act, grad_up_act)


def local(acts, gate_codes, gate_scales, up_codes, up_scales, down_codes, down_scales, cotangent):
    w_gate = dequantize(gate_codes, gate_scales)
    w_up = dequantize(up_codes, up_scales)
    w_down = dequantize(down_codes, down_scales)
    gathered = lax.all_gather(acts, "fsdp", axis=0, tiled=True)
    gate_part = contract_last(gathered, w_gate)
    up_part = contract_last(gathered, w_up)
    gate, up = (
        lax.psum(gate_part.astype(jnp.bfloat16), "tp").astype(jnp.float32),
        lax.psum(up_part.astype(jnp.bfloat16), "tp").astype(jnp.float32),
    )
    hidden = (jax.nn.silu(gate) * up).astype(jnp.bfloat16)
    output = lax.psum_scatter(
        jnp.dot(hidden, w_down, preferred_element_type=jnp.float32).astype(jnp.bfloat16),
        "fsdp",
        scatter_dimension=0,
        tiled=True,
    )
    cot_rows = lax.all_gather(cotangent, "fsdp", axis=0, tiled=True)
    grad_part = contract_last(cot_rows, w_down)
    grad_hidden = lax.psum(grad_part.astype(jnp.bfloat16), "tp").astype(jnp.float32)
    grad_gate_act, grad_up_act = local_grads(grad_hidden, gate, up)
    grad_gate = contract_first(grad_gate_act, gathered)
    grad_up = contract_first(grad_up_act, gathered)
    grad_down = contract_first(hidden, cot_rows)
    return (output, grad_gate, grad_up, grad_down)


def solution(mesh):
    in_specs = (
        P("fsdp", "tp"),
        P("fsdp", "tp"),
        P("fsdp", "tp"),
        P("fsdp", "tp"),
        P("fsdp", "tp"),
        P("fsdp", "tp"),
        P("fsdp", "tp"),
        P("fsdp", "tp"),
    )
    out_specs = (P("fsdp", "tp"), P("fsdp", "tp"), P("fsdp", "tp"), P("fsdp", "tp"))
    return jax.shard_map(local, mesh=mesh, in_specs=in_specs, out_specs=out_specs, check_vma=False)
```

profile of v0, /device:TPU:0, one launch (start us, length us, event | category | flops | bytes accessed | tf_op | source)
XLA Modules:
  0.0 760.6 jit_solution(13742724389807997441)
XLA Ops:
  7.2 0.0 copy-start.3
  7.2 0.0 all-gather.3.cloned.1.call-start
  7.2 0.7 all-gather.3.cloned.1.call-update
  7.9 0.0 all-gather.5.cloned.1.call-start
  8.0 0.7 all-gather.5.cloned.1.call-update
  8.7 0.0 all-reduce.3.cloned.1.call-start
  8.7 0.8 copy.12
  9.6 0.8 copy.13
  10.4 0.9 copy.14
  11.3 0.5 mul.64
  11.8 2.0 fusion.16
  13.8 165.5 %all-gather.3.cloned.1.call-done = bf16[4096,1024]{1,0:T(8,128)(2,1)} async-done(((bf16[128,1024]{1,0:T(8,128)(2,1)}), bf16[4096,1024]{1,0:T(8,128)(2,1)}) %all-gather.3.cloned.1.call-update) | async-done | bytes 8388624 | tf_op jit(solution)/shard_map/all_gather | solution.py:45
  179.3 0.0 slice-start
  179.3 0.5 mul.56
  179.8 0.0 copy-done.3
  179.9 0.0 slice-start.1
  179.9 0.0 copy-start.4
  179.9 10.2 %fusion.9 = bf16[4096,448]{0,1:T(8,128)(2,1)} fusion(bf16[4096,1024]{1,0:T(8,128)(2,1)} %all-gather.3.cloned.1.call-done, f32[56,8,8,128]{3,2,1,0:T(8,128)S(1)} %bitcast.32, s32[448,1024]{1,0:T(8,128)S(1)} %copy-done.3), kind=kOutput, calls=%fused_computation.19 | convolution fusion | flops 3761307648 | bytes 15728640 | tf_op jit(solution)/shard_map/dot_general | solution.py:19
  190.1 0.5 mul.60
  190.6 0.0 slice-done
  190.6 0.0 slice-done.1
  190.6 0.0 copy-done.4
  190.6 5.6 fusion.10
  196.2 152.9 %all-gather.5.cloned.1.call-done = bf16[4096,1024]{1,0:T(8,128)(2,1)} async-done(((bf16[128,1024]{1,0:T(8,128)(2,1)}), bf16[4096,1024]{1,0:T(8,128)(2,1)}) %all-gather.5.cloned.1.call-update) | async-done | bytes 8388624 | tf_op jit(solution)/shard_map/all_gather | solution.py:59
  349.1 9.9 %fusion.11 = bf16[4096,448]{0,1:T(8,128)(2,1)} fusion(bf16[448,1024]{1,0:T(8,128)(2,1)S(1)} %fusion.16, bf16[4096,1024]{1,0:T(8,128)(2,1)} %all-gather.5.cloned.1.call-done), kind=kOutput, calls=%fused_computation.21 | convolution fusion | flops 3759931392 | bytes 12976128 | tf_op jit(solution)/shard_map/dot_general | solution.py:19
  359.0 0.0 all-reduce.3.cloned.1.call-update
  359.1 0.0 reduce-scatter.2.cloned.1.call-start
  359.1 204.4 %all-reduce.3.cloned.1.call-done = (bf16[4096,448]{0,1:T(8,128)(2,1)}, bf16[4096,448]{0,1:T(8,128)(2,1)}, bf16[4096,448]{0,1:T(8,128)(2,1)}) async-done(((bf16[4096,448]{0,1:T(8,128)(2,1)}, bf16[4096,448]{0,1:T(8,128)(2,1)}, bf16[4096,448]{0,1:T(8,128)(2,1)}), (bf16[4096,448]{0,1:T(8,128)(2,1)}, bf16[4096,448]{0,1:T(8,128)(2,1)}, bf16[4096,448]{0,1:T(8,128)(2,1)})) %all-reduce.3.cloned.1.call-update) | async-done | bytes 11010064 | tf_op jit(solution)/shard_map/psum | solution.py:50
  563.5 11.5 %convolution_convert_fusion = bf16[4096,1024]{1,0:T(8,128)(2,1)} fusion(bf16[448,1024]{1,0:T(8,128)(2,1)S(1)} %fusion.16, bf16[4096,448]{0,1:T(8,128)(2,1)} %get-tuple-element.4, bf16[4096,448]{0,1:T(8,128)(2,1)} %get-tuple-element.5), kind=kOutput, calls=%fused_computation.6 | convolution fusion | flops 3776970752 | bytes 16646144 | tf_op jit(solution)/shard_map/dot_general | solution.py:54
  575.1 0.0 reduce-scatter.2.cloned.1.call-update
  575.1 0.0 copy-start.1
  575.1 0.0 copy-start.2
  575.1 0.0 slice-start.2
  575.1 11.5 %fusion.23 = f32[448,1024]{1,0:T(8,128)} fusion(bf16[4096,1024]{1,0:T(8,128)(2,1)} %all-gather.5.cloned.1.call-done, bf16[4096,448]{0,1:T(8,128)(2,1)} %get-tuple-element.4, bf16[4096,448]{0,1:T(8,128)(2,1)} %get-tuple-element.5), kind=kOutput, calls=%fused_computation.32 | convolution fusion | flops 3772776448 | bytes 17563648 | tf_op jit(solution)/shard_map/dot_general | solution.py:25
  586.6 0.0 slice-start.3
  586.6 0.0 copy-done.1
  586.6 0.0 copy-done.2
  586.7 0.0 copy-start
  586.7 9.4 %fusion.12 = f32[448,1024]{1,0:T(8,128)} fusion(bf16[4096,1024]{1,0:T(8,128)(2,1)} %all-gather.3.cloned.1.call-done, bf16[4096,448]{0,1:T(8,128)(2,1)S(1)} %copy-done.2, bf16[4096,448]{0,1:T(8,128)(2,1)S(1)} %copy-done.1), kind=kOutput, calls=%fused_computation.22 | convolution fusion | flops 3772776448 | bytes 17563648 | tf_op jit(solution)/shard_map/dot_general | solution.py:25
  596.1 0.0 slice-done.2
  596.1 0.0 slice-done.3
  596.1 0.0 copy-done
  596.1 6.9 fusion.14
  603.0 151.1 %reduce-scatter.2.cloned.1.call-done = bf16[128,1024]{1,0:T(8,128)(2,1)} async-done(((bf16[4096,1024]{1,0:T(8,128)(2,1)}), bf16[128,1024]{1,0:T(8,128)(2,1)}) %reduce-scatter.2.cloned.1.call-update) | async-done | bytes 262160 | tf_op jit(solution)/shard_map/reduce_scatter | solution.py:53
  (2 shorter events, 0.0 us)
Async XLA Ops:
  7.2 172.7 %copy-start.3 = (s32[448,1024]{1,0:T(8,128)S(1)}, s32[448,1024]{1,0:T(8,128)}, u32[]{:S(2)}) copy-start(s32[448,1024]{1,0:T(8,128)} %param.9) | copy-start | bytes 5505028
  7.2 172.1 %all-gather.3.cloned.1.call-start = ((), (), s32[]{:S(2)}) async-start(), calls=%async_computation.1 | async-start | bytes 8650752 | tf_op jit(solution)/shard_map/all_gather | solution.py:45
  7.9 341.2 %all-gather.5.cloned.1.call-start = ((), (), s32[]{:S(2)}) async-start(), calls=%async_computation.3 | async-start | bytes 8650752 | tf_op jit(solution)/shard_map/all_gather | solution.py:59
  8.7 554.9 %all-reduce.3.cloned.1.call-start = ((), (), s32[]{:S(2)}) async-start(), calls=%async_computation.4 | async-start | bytes 22020096 | tf_op jit(solution)/shard_map/psum | solution.py:50
  179.3 11.3 %slice-start = ((s8[8388608]{0:T(1024)(128)(4,1)}), s8[4194304]{0:T(1024)(128)(4,1)S(1)}, s32[]{:S(2)}) async-start(s8[8388608]{0:T(1024)(128)(4,1)} %bitcast.34), calls=%async_computation.5 | async-start | bytes 8388608
  179.9 10.8 %slice-start.1 = ((s8[8388608]{0:T(1024)(128)(4,1)}), s8[4194304]{0:T(1024)(128)(4,1)S(1)}, s32[]{:S(2)}) async-start(s8[8388608]{0:T(1024)(128)(4,1)} %bitcast.34), calls=%async_computation.6 | async-start | bytes 8388608
  179.9 10.8 %copy-start.4 = (s32[448,1024]{1,0:T(8,128)S(1)}, s32[448,1024]{1,0:T(8,128)}, u32[]{:S(2)}) copy-start(s32[448,1024]{1,0:T(8,128)} %param.11) | copy-start | bytes 5505028
  359.1 395.0 %reduce-scatter.2.cloned.1.call-start = ((), (), s32[]{:S(2)}) async-start(), calls=%async_computation.2 | async-start | bytes 8650752 | tf_op jit(solution)/shard_map/reduce_scatter | solution.py:53
  575.1 11.6 %copy-start.1 = (bf16[4096,448]{0,1:T(8,128)(2,1)S(1)}, bf16[4096,448]{0,1:T(8,128)(2,1)}, u32[]{:S(2)}) copy-start(bf16[4096,448]{0,1:T(8,128)(2,1)} %get-tuple-element.5) | copy-start | bytes 11010052
  575.1 11.6 %copy-start.2 = (bf16[4096,448]{0,1:T(8,128)(2,1)S(1)}, bf16[4096,448]{0,1:T(8,128)(2,1)}, u32[]{:S(2)}) copy-start(bf16[4096,448]{0,1:T(8,128)(2,1)} %get-tuple-element.6) | copy-start | bytes 11010052
  575.1 21.0 %slice-start.2 = ((s8[8388608]{0:T(1024)(128)(4,1)}), s8[4194304]{0:T(1024)(128)(4,1)S(1)}, s32[]{:S(2)}) async-start(s8[8388608]{0:T(1024)(128)(4,1)} %bitcast.36), calls=%async_computation.7 | async-start | bytes 8388608
  586.6 9.4 %slice-start.3 = ((s8[8388608]{0:T(1024)(128)(4,1)}), s8[4194304]{0:T(1024)(128)(4,1)S(1)}, s32[]{:S(2)}) async-start(s8[8388608]{0:T(1024)(128)(4,1)} %bitcast.36), calls=%async_computation.8 | async-start | bytes 8388608
  586.7 9.4 %copy-start = (bf16[4096,448]{0,1:T(8,128)(2,1)S(1)}, bf16[4096,448]{0,1:T(8,128)(2,1)}, u32[]{:S(2)}) copy-start(bf16[4096,448]{0,1:T(8,128)(2,1)} %get-tuple-element.4) | copy-start | bytes 11010052
Sparse Core Ops, SparseCore 0:
  9.7 169.6 all-gather.2
  180.9 168.0 all-gather.4
  359.2 204.3 all-reduce.2
  575.2 178.8 reduce-scatter.1
where the time goes:
time: 761 us
  waiting for transfers between devices  675 us (89%)
  matrix products  65.1 us (9%)
  between operations  13.9 us (2%)
    psum x1, waiting for transfers between devices, local(): lax.psum(up_part.astype(jnp.bfloat16), 'tp').astype(jnp.float32)  204 us
    all_gather x1, waiting for transfers between devices, local(): gathered = lax.all_gather(acts, 'fsdp', axis=0, tiled=True)  165 us
    all_gather x1, waiting for transfers between devices, local(): cot_rows = lax.all_gather(cotangent, 'fsdp', axis=0, tiled=True)  153 us
    reduce_scatter x1, waiting for transfers between devices, local(): lax.psum_scatter(jnp.dot(hidden, w_down, preferred_element_type=jnp.float...  151 us
    dot_general x3, matrix products, contract_first(): lax.dot_general(left_side, right_side, (((0,), (0,)), ((), ())), preferre...  27.8 us
    dot_general x3, matrix products, contract_last(): lax.dot_general(left_side, right_side, (((1,), (1,)), ((), ())), preferre...  25.7 us
  transfers between devices with their start and end apart: 4, of which 4 were waited for; matrix products, arithmetic and copies ran while one was open for 7% of the time, Pallas kernels for 0%

commit v1 on v0

v1 whole, which is shorter than its diff:
```python
import functools

import jax
import jax.numpy as jnp
from jax import lax
from jax.experimental import pallas as pl
from jax.experimental.pallas import tpu as pltpu
from jax.sharding import PartitionSpec as P

MESH = pl.DeviceIdType.MESH
F32, BF16 = jnp.float32, jnp.bfloat16
GROUP = 128
HID = 448
HALF = 1024
WIDE = 2 * HALF
BLK = 64
CH = 256
DELTAS = (1, 3, 2)

ACTS, COT, WTS, TFGU, TFGH, RSB, RSA, RSY, OUTS, GRD, GRU, NSEM = 0, 14, 28, 31, 39, 47, 53, 56, 57, 58, 59, 60
SIB, YLO, AOWN, ALO, BH = 0, 1, 2, 5, 8


def nt(left, right):
    return lax.dot_general(left, right, (((1,), (1,)), ((), ())), preferred_element_type=F32)


def nn(left, right):
    return lax.dot_general(left, right, (((1,), (0,)), ((), ())), preferred_element_type=F32)


def kernel(acts, gc, gs, uc, us, dc, ds, cot, out, gg, gu, gd,
           A, C, W2, WD, TO, TR, O, RB, RA, RY, HT, DS, DR, ssem, rsem, lsem, credit):
    f, t = lax.axis_index("fsdp"), lax.axis_index("tp")
    x, ylo, z = f % 4, (f // 4) % 2, f // 8
    yhi, c = t // 2, t % 2
    a = x * (1 - c) + z * c
    b = z * (1 - c) + x * c

    def dev(x_, ylo_, z_, yhi_, c_):
        return (z_ * 8 + ylo_ * 4 + x_, yhi_ * 2 + c_)

    def apeer(d):
        return dev((x + d * (1 - c)) % 4, ylo, (z + d * c) % 4, yhi, c)

    def bpeer(d):
        return dev((x + d * c) % 4, ylo, (z + d * (1 - c)) % 4, yhi, c)

    sib = dev(x, ylo, z, yhi, 1 - c)
    lo = dev(x, 1 - ylo, z, yhi, c)
    hi = dev(x, ylo, z, 1 - yhi, c)

    def rc(src, dst, s, r, to):
        return pltpu.make_async_remote_copy(src_ref=src, dst_ref=dst, send_sem=ssem.at[s], recv_sem=rsem.at[r],
                                            device_id=to, device_id_type=MESH)

    def send(src, dst, s, r, to):
        rc(src, dst, s, r, to).start()

    def got(dst, r, to):
        rc(dst, dst, 0, r, to).wait_recv()

    def sent(src, s, to):
        rc(src, src, s, 0, to).wait_send()

    def blk(a_, ylo_):
        return pl.ds(pl.multiple_of(((b * 4 + a_) * 2 + ylo_) * BLK, BLK), BLK)

    def pair(a_):
        return pl.ds(pl.multiple_of((b * 4 + a_) * 2 * BLK, 2 * BLK), 2 * BLK)

    def chunk(b_, h):
        return b_ * 2 + h

    def rows(k):
        return pl.ds(pl.multiple_of(k * CH, CH), CH)

    def bd(j):
        return (b + 1 + 2 * j - 3 * (j // 2)) % 4

    mine = pl.ds(pl.multiple_of(c * BLK, BLK), BLK)
    theirs = pl.ds(pl.multiple_of((1 - c) * BLK, BLK), BLK)
    own = blk(a, ylo)
    other = blk(a, 1 - ylo)
    sibs = pl.ds(pl.multiple_of(((a * 4 + b) * 2 + ylo) * BLK, BLK), BLK)

    def local(src, dst, i):
        return pltpu.make_async_copy(src, dst, lsem.at[i])

    def opening(codes, scales):
        loads = [local(gc, codes.at[0], 0), local(gs, scales.at[0], 1), local(uc, codes.at[1], 2), local(us, scales.at[1], 3),
                 local(ds, scales.at[2], 4)]
        own_acts = local(acts.at[mine, :], A.at[own, 0:HALF], 5)
        own_cot = local(cot.at[mine, :], C.at[own, 0:HALF], 6)
        for load in (own_acts, loads[0], loads[1], own_cot, loads[2], loads[3], loads[4]):
            load.start()

        barrier = pltpu.get_barrier_semaphore()
        peers = [sib, lo, hi] + [apeer(d) for d in DELTAS] + [bpeer(d) for d in DELTAS]
        for peer in peers:
            pl.semaphore_signal(barrier, inc=1, device_id=peer, device_id_type=MESH)
        pl.semaphore_wait(barrier, len(peers))

        send(acts.at[theirs, :], A.at[sibs, HALF:WIDE], ACTS + SIB, ACTS + SIB, sib)
        send(cot.at[theirs, :], C.at[sibs, HALF:WIDE], COT + SIB, COT + SIB, sib)
        own_acts.wait()
        got(A.at[own, HALF:WIDE], ACTS + SIB, sib)
        send(A.at[own, :], A.at[own, :], ACTS + YLO, ACTS + YLO, lo)
        for d in DELTAS:
            send(A.at[own, :], A.at[own, :], ACTS + AOWN + d - 1, ACTS + AOWN + 3 - d, apeer(d))
        own_cot.wait()
        got(C.at[own, HALF:WIDE], COT + SIB, sib)
        send(C.at[own, :], C.at[own, :], COT + YLO, COT + YLO, lo)

        def dequantize(slot, which, w, first):
            def tile(i, _):
                r = pl.ds(pl.multiple_of(i * 32, 32), 32)
                rw = pl.ds(pl.multiple_of(first + i * 32, 32), 32)
                for g in range(HALF // GROUP):
                    cols = slice(g * GROUP, (g + 1) * GROUP)
                    w[rw, cols] = (codes[slot, r, cols].astype(F32) * scales[which, r, g:g + 1]).astype(BF16)
                return 0

            lax.fori_loop(0, HID // 32, tile, 0)

        down = local(dc, codes.at[0], 7)
        loads[0].wait()
        loads[1].wait()
        dequantize(0, 0, W2, 0)
        send(W2.at[0:HID, 0:HALF], W2.at[0:HID, HALF:WIDE], WTS, WTS, sib)
        down.start()
        loads[2].wait()
        loads[3].wait()
        dequantize(1, 1, W2, HID)
        send(W2.at[HID:2 * HID, 0:HALF], W2.at[HID:2 * HID, HALF:WIDE], WTS + 1, WTS + 1, sib)
        got(A.at[other, :], ACTS + YLO, lo)
        for d in DELTAS:
            send(A.at[other, :], A.at[other, :], ACTS + ALO + d - 1, ACTS + ALO + 3 - d, apeer(d))
        loads[4].wait()
        down.wait()
        dequantize(0, 2, WD, 0)
        send(WD.at[:, 0:HALF], WD.at[:, HALF:WIDE], WTS + 2, WTS + 2, sib)

    pl.run_scoped(opening, pltpu.VMEM((2, HID, HALF), jnp.int32), pltpu.VMEM((3, HID, HALF // GROUP), F32))

    def gate_up(k):
        block = A[rows(k), :]
        for part in range(2):
            r = slice(part * HID, (part + 1) * HID)
            TO[k, r, :] = nt(W2[r, :], block).astype(BF16)
        send(TO.at[k, 0:2 * HID, :], TR.at[k, 0:2 * HID, :], TFGU + k, TFGU + k, hi)

    def grad_hidden(k):
        TO[k, 2 * HID:3 * HID, :] = nt(WD[...], C[rows(k), :]).astype(BF16)

    def send_grad_hidden(k):
        send(TO.at[k, 2 * HID:3 * HID, :], TR.at[k, 2 * HID:3 * HID, :], TFGH + k, TFGH + k, hi)

    for d in DELTAS:
        got(A.at[blk((a + d) % 4, ylo), :], ACTS + AOWN + d - 1, apeer(d))
        got(A.at[blk((a + d) % 4, 1 - ylo), :], ACTS + ALO + d - 1, apeer(d))

    def bsend(buf, base, h, d):
        r = rows(chunk(b, h))
        send(buf.at[r, :], buf.at[r, :], base + BH + 3 * h + d - 1, base + BH + 3 * h + 3 - d, bpeer(d))

    def bgot(buf, base, h, d):
        got(buf.at[rows(chunk((b + d) % 4, h)), :], base + BH + 3 * h + d - 1, bpeer(d))

    for d in DELTAS:
        bsend(A, ACTS, 0, d)
    for part in range(2):
        got(W2.at[part * HID:(part + 1) * HID, HALF:WIDE], WTS + part, sib)

    def first(h, _):
        gate_up(chunk(b, h))
        return 0

    lax.fori_loop(0, 2, first, 0)

    def second(j, _):
        d = 1 + 2 * j - 3 * (j // 2)
        bgot(A, ACTS, 0, d)
        bsend(A, ACTS, 1, d)
        gate_up(chunk((b + d) % 4, 0))
        return 0

    lax.fori_loop(0, 3, second, 0)
    got(C.at[other, :], COT + YLO, lo)

    def third(j, _):
        d = 1 + 2 * j - 3 * (j // 2)
        bgot(A, ACTS, 1, d)
        send(C.at[pair(a), :], C.at[pair(a), :], COT + AOWN + d - 1, COT + AOWN + 3 - d, apeer(d))
        gate_up(chunk((b + d) % 4, 1))
        return 0

    lax.fori_loop(0, 3, third, 0)

    for part in range(2):
        sent(W2.at[part * HID:(part + 1) * HID, 0:HALF], WTS + part, sib)
    pl.semaphore_signal(credit, inc=1, device_id=sib, device_id_type=MESH)

    for d in DELTAS:
        got(C.at[pair((a + d) % 4), :], COT + AOWN + d - 1, apeer(d))
    for d in DELTAS:
        bsend(C, COT, 0, d)
    got(WD.at[:, HALF:WIDE], WTS + 2, sib)

    def activate(k):
        got(TR.at[k, 0:2 * HID, :], TFGU + k, hi)
        sent(TO.at[k, 0:2 * HID, :], TFGU + k, hi)

        def tile(i, _):
            r = pl.ds(pl.multiple_of(i * 32, 32), 32)
            q = pl.ds(pl.multiple_of(HID + i * 32, 32), 32)
            gate = TO[k, r, :].astype(F32) + TR[k, r, :].astype(F32)
            up = TO[k, q, :].astype(F32) + TR[k, q, :].astype(F32)
            s = 1.0 / (1.0 + jnp.exp(-gate))
            silu = gate * s
            TO[k, r, :] = (silu * up).astype(BF16)
            TR[k, r, :] = silu.astype(BF16)
            TR[k, q, :] = (up * (s * (1.0 + gate * (1.0 - s)))).astype(BF16)
            return 0

        lax.fori_loop(0, HID // 32, tile, 0)

    def transpose(k):
        HT[...] = jnp.transpose(TO[k, 0:HID, :].astype(F32)).astype(BF16)

    def output_part(h, d):
        k = chunk((b + d) % 4, h)
        activate(k)
        transpose(k)
        o = pl.ds(pl.multiple_of(((d - 1) * 2 + h) * CH, CH), CH)

        def tile(i, _):
            cols = pl.ds(pl.multiple_of(i * 512, 512), 512)
            O[o, cols] = nn(HT[...], WD[:, cols]).astype(BF16)
            return 0

        lax.fori_loop(0, WIDE // 512, tile, 0)
        to = pl.ds(pl.multiple_of(((3 - d) * 2 + h) * CH, CH), CH)
        send(O.at[o, :], RB.at[to, :], RSB + (d - 1) * 2 + h, RSB + (3 - d) * 2 + h, bpeer(d))

    def own_hidden(h, _):
        activate(chunk(b, h))
        return 0

    lax.fori_loop(0, 2, own_hidden, 0)

    def own_grad_hidden(h, _):
        grad_hidden(chunk(b, h))
        return 0

    lax.fori_loop(0, 2, own_grad_hidden, 0)

    def fourth(j, _):
        d = 1 + 2 * j - 3 * (j // 2)
        output_part(0, d)
        bgot(C, COT, 0, d)
        bsend(C, COT, 1, d)
        grad_hidden(chunk((b + d) % 4, 0))
        return 0

    lax.fori_loop(0, 3, fourth, 0)

    def fifth(j, _):
        d = 1 + 2 * j - 3 * (j // 2)
        output_part(1, d)
        bgot(C, COT, 1, d)
        grad_hidden(chunk((b + d) % 4, 1))
        send_grad_hidden(chunk(bd(j), 0))
        return 0

    lax.fori_loop(0, 3, fifth, 0)

    def sixth(j, _):
        send_grad_hidden(chunk(bd(j), 1))
        return 0

    lax.fori_loop(0, 3, sixth, 0)
    for h in range(2):
        send_grad_hidden(chunk(b, h))

    def closing(gsum, dsum):
        gsum[...] = jnp.zeros_like(gsum)
        dsum[...] = jnp.zeros_like(dsum)

        def down_step(k, _):
            def tile(i, _):
                cols = pl.ds(pl.multiple_of(i * 512, 512), 512)
                dsum[:, cols] += nn(TO[k, 0:HID, :], C[rows(k), cols])
                return 0

            return lax.fori_loop(0, WIDE // 512, tile, 0)

        lax.fori_loop(0, 8, down_step, 0)

        def narrow(i, _):
            r = pl.ds(pl.multiple_of(i * 32, 32), 32)
            DS[r, :] = dsum[r, HALF:WIDE].astype(BF16)
            return 0

        lax.fori_loop(0, HID // 32, narrow, 0)
        send(DS, DR, GRD, GRD, sib)

        def slopes(k):
            got(TR.at[k, 2 * HID:3 * HID, :], TFGH + k, hi)

            def tile(i, _):
                r = pl.ds(pl.multiple_of(i * 32, 32), 32)
                q = pl.ds(pl.multiple_of(HID + i * 32, 32), 32)
                w = pl.ds(pl.multiple_of(2 * HID + i * 32, 32), 32)
                grad = TO[k, w, :].astype(F32) + TR[k, w, :].astype(F32)
                TR[k, r, :] = (grad * TR[k, r, :].astype(F32)).astype(BF16)
                TR[k, q, :] = (grad * TR[k, q, :].astype(F32)).astype(BF16)
                return 0

            lax.fori_loop(0, HID // 32, tile, 0)

        def weigh(k, low, high):
            def tile(i, _):
                cols = pl.ds(pl.multiple_of(i * 256, 256), 256)
                gsum[:, cols] += nn(TR[k, 0:2 * HID, :], A[rows(k), cols])
                return 0

            lax.fori_loop(low, high, tile, 0)

        def gate_step(k):
            slopes(k)
            weigh(k, 0, WIDE // 256)

        def remote_step(j, h):
            gate_step(chunk(bd(j), h))

        lax.fori_loop(0, 3, lambda j, _: (remote_step(j, 0), 0)[1], 0)

        for d in DELTAS:
            for h in range(2):
                s = (d - 1) * 2 + h
                got(RB.at[s * CH:(s + 1) * CH, :], RSB + s, bpeer(d))

        def badd(h, _):
            transpose(chunk(b, h))
            r = [pl.ds(pl.multiple_of((2 * i + h) * CH, CH), CH) for i in range(3)]

            def tile(i, _):
                cols = pl.ds(pl.multiple_of(i * 256, 256), 256)
                total = nn(HT[...], WD[:, cols])
                for q in r:
                    total = total + RB[q, cols].astype(F32)
                RB[r[0], cols] = total.astype(BF16)
                return 0

            return lax.fori_loop(0, WIDE // 256, tile, 0)

        lax.fori_loop(0, 2, badd, 0)

        def part(a_):
            return pl.ds(pl.multiple_of(a_ * 2 * BLK, 2 * BLK), 2 * BLK)

        def slot(d):
            return pl.ds((d - 1) * 2 * BLK, 2 * BLK)

        for d in DELTAS:
            send(RB.at[part((a + d) % 4), :], RA.at[slot(4 - d), :], RSA + d - 1, RSA + 3 - d, apeer(d))
        lax.fori_loop(0, 2, lambda j, _: (remote_step(j, 1), 0)[1], 0)

        for d in DELTAS:
            got(RA.at[slot(d), :], RSA + d - 1, apeer(d))

        def aadd(i, _):
            cols = pl.ds(pl.multiple_of(i * 256, 256), 256)
            total = RB[part(a), cols].astype(F32)
            for d in DELTAS:
                total = total + RA[slot(d), cols].astype(F32)
            RB[part(a), cols] = total.astype(BF16)
            return 0

        lax.fori_loop(0, WIDE // 256, aadd, 0)

        def half(ylo_):
            return pl.ds(pl.multiple_of((a * 2 + ylo_) * BLK, BLK), BLK)

        send(RB.at[half(1 - ylo), :], RY, RSY, RSY, lo)
        remote_step(2, 1)
        gate_step(chunk(b, 0))

        got(RY, RSY, lo)
        RB[half(ylo), :] = (RB[half(ylo), :].astype(F32) + RY[...].astype(F32)).astype(BF16)
        send(RB.at[half(ylo), HALF:WIDE], out.at[mine, :], OUTS, OUTS, sib)
        keep = local(RB.at[half(ylo), 0:HALF], out.at[mine, :], 0)
        keep.start()

        got(DR, GRD, sib)

        def down_add(i, _):
            r = pl.ds(pl.multiple_of(i * 32, 32), 32)
            dsum[r, 0:HALF] += DR[r, :].astype(F32)
            return 0

        lax.fori_loop(0, HID // 32, down_add, 0)
        put_down = local(dsum.at[:, 0:HALF], gd, 1)
        put_down.start()

        last = chunk(b, 1)
        slopes(last)
        weigh(last, HALF // 256, WIDE // 256)
        pl.semaphore_wait(credit, 1)

        def narrow_gates(i, _):
            r = pl.ds(pl.multiple_of(i * 32, 32), 32)
            W2[r, 0:HALF] = gsum[r, HALF:WIDE].astype(BF16)
            return 0

        lax.fori_loop(0, 2 * HID // 32, narrow_gates, 0)
        send(W2.at[:, 0:HALF], W2.at[:, HALF:WIDE], GRU, GRU, sib)
        weigh(last, 0, HALF // 256)
        got(W2.at[:, HALF:WIDE], GRU, sib)

        def gates_add(i, _):
            r = pl.ds(pl.multiple_of(i * 32, 32), 32)
            gsum[r, 0:HALF] += W2[r, HALF:WIDE].astype(F32)
            return 0

        lax.fori_loop(0, 2 * HID // 32, gates_add, 0)
        put_up = local(gsum.at[0:HID, 0:HALF], gu, 2)
        put_gate = local(gsum.at[HID:2 * HID, 0:HALF], gg, 3)
        put_up.start()
        put_gate.start()

        sent(acts.at[theirs, :], ACTS + SIB, sib)
        sent(cot.at[theirs, :], COT + SIB, sib)
        sent(A.at[own, :], ACTS + YLO, lo)
        sent(C.at[own, :], COT + YLO, lo)
        for d in DELTAS:
            sent(A.at[own, :], ACTS + AOWN + d - 1, apeer(d))
            sent(A.at[other, :], ACTS + ALO + d - 1, apeer(d))
            sent(C.at[pair(a), :], COT + AOWN + d - 1, apeer(d))
            sent(RB.at[part((a + d) % 4), :], RSA + d - 1, apeer(d))
            for h in range(2):
                r = rows(chunk(b, h))
                sent(A.at[r, :], ACTS + BH + 3 * h + d - 1, bpeer(d))
                sent(C.at[r, :], COT + BH + 3 * h + d - 1, bpeer(d))
                s = (d - 1) * 2 + h
                sent(O.at[s * CH:(s + 1) * CH, :], RSB + s, bpeer(d))
        sent(WD.at[:, 0:HALF], WTS + 2, sib)
        for k in range(8):
            sent(TO.at[k, 2 * HID:3 * HID, :], TFGH + k, hi)
        sent(RB.at[half(1 - ylo), :], RSY, lo)
        sent(RB.at[half(ylo), HALF:WIDE], OUTS, sib)
        sent(DS, GRD, sib)
        sent(W2.at[:, 0:HALF], GRU, sib)
        got(out.at[theirs, :], OUTS, sib)
        keep.wait()
        put_down.wait()
        put_up.wait()
        put_gate.wait()

    pl.run_scoped(closing, pltpu.VMEM((2 * HID, WIDE), F32), pltpu.VMEM((HID, WIDE), F32))


def local_step(acts, gc, gs, uc, us, dc, ds, cot):
    anywhere = pl.BlockSpec(memory_space=pl.ANY)
    out, gg, gu, gd = pl.pallas_call(
        kernel,
        out_shape=(
            jax.ShapeDtypeStruct((2 * BLK, HALF), BF16),
            jax.ShapeDtypeStruct((HID, HALF), F32),
            jax.ShapeDtypeStruct((HID, HALF), F32),
            jax.ShapeDtypeStruct((HID, HALF), F32),
        ),
        in_specs=[anywhere] * 8,
        out_specs=(anywhere,) * 4,
        scratch_shapes=[
            pltpu.VMEM((8 * CH, WIDE), BF16),
            pltpu.VMEM((8 * CH, WIDE), BF16),
            pltpu.VMEM((2 * HID, WIDE), BF16),
            pltpu.VMEM((HID, WIDE), BF16),
            pltpu.VMEM((8, 3 * HID, CH), BF16),
            pltpu.VMEM((8, 3 * HID, CH), BF16),
            pltpu.VMEM((6 * CH, WIDE), BF16),
            pltpu.VMEM((6 * CH, WIDE), BF16),
            pltpu.VMEM((6 * BLK, WIDE), BF16),
            pltpu.VMEM((BLK, WIDE), BF16),
            pltpu.VMEM((CH, HID), BF16),
            pltpu.VMEM((HID, HALF), BF16),
            pltpu.VMEM((HID, HALF), BF16),
            pltpu.SemaphoreType.DMA((NSEM,)),
            pltpu.SemaphoreType.DMA((NSEM,)),
            pltpu.SemaphoreType.DMA((8,)),
            pltpu.SemaphoreType.REGULAR,
        ],
        compiler_params=pltpu.CompilerParams(collective_id=0, has_side_effects=True, vmem_limit_bytes=63 << 20),
        name="swiglu_step",
    )(acts, gc, gs, uc, us, dc, ds, cot)
    return out, gg, gu, gd


def solution(mesh):
    spec = P("fsdp", "tp")
    return jax.shard_map(local_step, mesh=mesh, in_specs=(spec,) * 8, out_specs=(spec,) * 4, check_vma=False)
```

time: 761 us -> 244 us (0.32)
  waiting for transfers between devices: 675 us -> 0 us
  Pallas kernels: 0 us -> 227 us
  matrix products: 65.1 us -> 0 us
  between operations: 13.9 us -> 0.64 us
  local copies, waits for them, and re-layouts: 4.18 us -> 12.8 us
    all_gather x2 -> x0, waiting for transfers between devices: 318 us -> none  [the longest x1 165 us: local(): gathered = lax.all_gather(acts, 'fsdp', axis=0, tiled=True)]
    pallas_call x0 -> x1, Pallas kernels: none -> 227 us  [local_step(): pl.pallas_call(kernel, out_shape=(jax.ShapeDtypeStruct((2 * BLK, HALF), B...]
    psum x1 -> x0, waiting for transfers between devices: 204 us -> none  [local(): lax.psum(up_part.astype(jnp.bfloat16), 'tp').astype(jnp.float32)]
    reduce_scatter x1 -> x0, waiting for transfers between devices: 151 us -> none  [local(): lax.psum_scatter(jnp.dot(hidden, w_down, preferred_element_type=jnp.float...]
    dot_general x7 -> x0, matrix products: 65.1 us -> none  [the longest x3 27.8 us: contract_first(): lax.dot_general(left_side, right_side, (((0,), (0,)), ((), ())), preferre...]
    unnamed x21 -> x11, local copies, waits for them, and re-layouts: 2.58 us -> 12.8 us
  transfers between devices with their start and end apart: 4 -> 0, of which waited for: 4 -> 0; matrix products, arithmetic and copies ran while one was open for 7% -> 0% of each run, Pallas kernels for 0% -> 0%
where the time goes in v1:
time: 244 us; the launch traced here: 240 us
  Pallas kernels  227 us (93%)
  local copies, waits for them, and re-layouts  12.8 us (5%)
    pallas_call x1, Pallas kernels, local_step(): pl.pallas_call(kernel, out_shape=(jax.ShapeDtypeStruct((2 * BLK, HALF), B...  227 us
    unnamed x11, local copies, waits for them, and re-layouts  12.8 us

profile of v1, /device:TPU:0, one launch (start us, length us, event | category | flops | bytes accessed | tf_op | source)
XLA Modules:
  0.0 239.9 jit_solution(5395726518977422149)
XLA Ops:
  0.6 1.5 copy.12.gs
  2.2 1.5 copy.13.us
  3.7 1.5 copy.14.ds
  5.2 226.5 %swiglu_step.1 = (bf16[128,1024]{1,0:T(8,128)(2,1)}, f32[448,1024]{1,0:T(8,128)}, f32[448,1024]{1,0:T(8,128)}, f32[448,1024]{1,0:T(8,128)}) custom-call(bf16[128,1024]{1,0:T(8,128)(2,1)} %acts.1, s32[448,1024]{1,0:T(8,128)} %gc.1, f32[448,8]{1,0:T(8,128)} %copy.12.gs, s32[448,1024]{1,0:T(8,128)} %uc.1, f32[448,8]{1,0:T(8,128)} %copy.13.us, s32[448,1024]{1,0:T(8,128)} %dc.1, ...), custom_call_target="tpu_custom_call" | custom-call | tf_op jit(solution)/shard_map/swiglu_step/pallas_call | solution.py:466
  231.8 1.7 copy.19
  233.5 0.0 copy-start.1
  233.5 3.1 %copy.20 = f32[448,1024]{1,0:T(8,128)} copy(f32[448,1024]{1,0:T(8,128)} %get-tuple-element.9) | data formatting | bytes 3670016
  236.5 0.0 copy-done.1
  236.5 0.0 copy-start
  236.5 1.2 copy.21
  237.8 0.9 copy-done
  238.7 1.2 copy.22
Async XLA Ops:
  233.5 3.1 %copy-start.1 = (f32[448,1024]{1,0:T(8,128)S(1)}, f32[448,1024]{1,0:T(8,128)}, u32[]{:S(2)}) copy-start(f32[448,1024]{1,0:T(8,128)} %get-tuple-element.10) | copy-start | bytes 5505028
  236.5 2.2 copy-start

commit v2 on v1

v2 whole, which is shorter than its diff:
```python
import functools

import jax
import jax.numpy as jnp
from jax import lax
from jax.experimental import pallas as pl
from jax.experimental.pallas import tpu as pltpu
from jax.sharding import PartitionSpec as P

MESH = pl.DeviceIdType.MESH
F32, BF16 = jnp.float32, jnp.bfloat16
GROUP = 128
HID = 448
HALF = 1024
WIDE = 2 * HALF
BLK = 64
CH = 256

ACTS, COT, WTS, TFGU, TFGH, RSB, RSA, RSY, OUTS, GRD, GRU, NSEM = 0, 26, 52, 55, 63, 71, 77, 83, 84, 85, 86, 87
SIB, YLO, AOWN, ALO, BPAIR = 0, 1, 2, 6, 10


def nt(left, right):
    return lax.dot_general(left, right, (((1,), (1,)), ((), ())), preferred_element_type=F32)


def nn(left, right):
    return lax.dot_general(left, right, (((1,), (0,)), ((), ())), preferred_element_type=F32)


def kernel(acts, gc, gs, uc, us, dc, ds, cot, out, gg, gu, gd,
           A, C, W2, WD, TO, TR, O, RB, RA, RY, HT, DS, DR, ssem, rsem, lsem, credit):
    f, t = lax.axis_index("fsdp"), lax.axis_index("tp")
    x, ylo, z = f % 4, (f // 4) % 2, f // 8
    yhi, c = t // 2, t % 2
    a = x * (1 - c) + z * c
    b = z * (1 - c) + x * c

    def dev(x_, ylo_, z_, yhi_, c_):
        return (z_ * 8 + ylo_ * 4 + x_, yhi_ * 2 + c_)

    def apeer(d):
        return dev((x + d * (1 - c)) % 4, ylo, (z + d * c) % 4, yhi, c)

    def bpeer(d):
        return dev((x + d * c) % 4, ylo, (z + d * (1 - c)) % 4, yhi, c)

    sib = dev(x, ylo, z, yhi, 1 - c)
    lo = dev(x, 1 - ylo, z, yhi, c)
    hi = dev(x, ylo, z, 1 - yhi, c)

    def rc(src, dst, s, r, to):
        return pltpu.make_async_remote_copy(src_ref=src, dst_ref=dst, send_sem=ssem.at[s], recv_sem=rsem.at[r],
                                            device_id=to, device_id_type=MESH)

    def send(src, dst, s, r, to):
        rc(src, dst, s, r, to).start()

    def got(dst, r, to):
        rc(dst, dst, 0, r, to).wait_recv()

    def sent(src, s, to):
        rc(src, src, s, 0, to).wait_send()

    def span(row, n):
        return pl.ds(pl.multiple_of(row, n), n)

    def blk(a_, ylo_):
        return span(((b * 4 + a_) * 2 + ylo_) * BLK, BLK)

    def chunk(d, h):
        return ((b + d) % 4) * 2 + (a // 2 + h) % 2

    def rows(k):
        return pl.ds(pl.multiple_of(k * CH, CH), CH)

    mine = pl.ds(pl.multiple_of(c * BLK, BLK), BLK)
    theirs = pl.ds(pl.multiple_of((1 - c) * BLK, BLK), BLK)
    own = blk(a, ylo)
    other = blk(a, 1 - ylo)
    sibs = pl.ds(pl.multiple_of(((a * 4 + b) * 2 + ylo) * BLK, BLK), BLK)

    def local(src, dst, i):
        return pltpu.make_async_copy(src, dst, lsem.at[i])

    class Round:
        def __init__(self, buf, row, n, base, peer):
            self.buf, self.row, self.n, self.base, self.peer = buf, row, n, base, peer

        def view(self, d, half=None):
            if half is None:
                return self.buf.at[span(self.row(d), self.n), :]
            return self.buf.at[span(self.row(d) + half * (self.n // 2), self.n // 2), :]

        def start(self):
            send(self.view(0), self.view(0), self.base, self.base + 1, self.peer(1))
            send(self.view(0), self.view(0), self.base + 1, self.base, self.peer(3))

        def forward(self):
            got(self.view(1), self.base, self.peer(1))
            send(self.view(1, 0), self.view(1, 0), self.base + 2, self.base + 2, self.peer(3))
            got(self.view(3), self.base + 1, self.peer(3))
            send(self.view(3, 1), self.view(3, 1), self.base + 3, self.base + 3, self.peer(1))

        def finish(self):
            got(self.view(2, 0), self.base + 2, self.peer(1))
            got(self.view(2, 1), self.base + 3, self.peer(3))

        def drain(self):
            sent(self.view(0), self.base, self.peer(1))
            sent(self.view(0), self.base + 1, self.peer(3))
            sent(self.view(1, 0), self.base + 2, self.peer(3))
            sent(self.view(3, 1), self.base + 3, self.peer(1))

    opposite = (a + 2) % 4
    order = (a, a + 1 - 2 * (a % 2), opposite + 1 - 2 * (opposite % 2), opposite)

    def rounds(buf, base):
        def around_a(ylo_, sem):
            return Round(buf, lambda d: ((b * 4 + (a + d) % 4) * 2 + ylo_) * BLK, BLK, base + sem, apeer)

        def around_b(i):
            return Round(buf, lambda d: (((b + d) % 4) * 4 + order[i]) * 2 * BLK, 2 * BLK, base + BPAIR + 4 * i, bpeer)

        return [around_a(ylo, AOWN), around_a(1 - ylo, ALO)], [around_b(i) for i in range(4)]

    acts_a, acts_b = rounds(A, ACTS)
    cot_a, cot_b = rounds(C, COT)

    def opening(codes, scales, turned):
        loads = [local(gc, codes.at[0], 0), local(gs, turned.at[0], 1), local(uc, codes.at[1], 2), local(us, turned.at[1], 3),
                 local(ds, turned.at[2], 4)]
        own_acts = local(acts.at[mine, :], A.at[own, 0:HALF], 5)
        own_cot = local(cot.at[mine, :], C.at[own, 0:HALF], 6)
        for load in (own_acts, loads[0], loads[1], own_cot, loads[2], loads[3], loads[4]):
            load.start()

        barrier = pltpu.get_barrier_semaphore()
        peers = [sib, lo, hi, apeer(1), apeer(3), bpeer(1), bpeer(3)]
        for peer in peers:
            pl.semaphore_signal(barrier, inc=1, device_id=peer, device_id_type=MESH)
        pl.semaphore_wait(barrier, len(peers))

        send(acts.at[theirs, :], A.at[sibs, HALF:WIDE], ACTS + SIB, ACTS + SIB, sib)
        send(cot.at[theirs, :], C.at[sibs, HALF:WIDE], COT + SIB, COT + SIB, sib)
        own_acts.wait()
        got(A.at[own, HALF:WIDE], ACTS + SIB, sib)
        send(A.at[own, :], A.at[own, :], ACTS + YLO, ACTS + YLO, lo)
        acts_a[0].start()
        own_cot.wait()
        got(C.at[own, HALF:WIDE], COT + SIB, sib)
        send(C.at[own, :], C.at[own, :], COT + YLO, COT + YLO, lo)
        cot_a[0].start()

        def dequantize(slot, which, w, first):
            scales[which] = jnp.transpose(turned[which])

            def tile(i, _):
                r = span(i * 32, 32)
                rw = span(first + i * 32, 32)
                for g in range(HALF // GROUP):
                    cols = slice(g * GROUP, (g + 1) * GROUP)
                    w[rw, cols] = (codes[slot, r, cols].astype(F32) * scales[which, r, g:g + 1]).astype(BF16)
                return 0

            lax.fori_loop(0, HID // 32, tile, 0)

        down = local(dc, codes.at[0], 7)
        loads[0].wait()
        loads[1].wait()
        dequantize(0, 0, W2, 0)
        send(W2.at[0:HID, 0:HALF], W2.at[0:HID, HALF:WIDE], WTS, WTS, sib)
        down.start()
        acts_a[0].forward()
        loads[2].wait()
        loads[3].wait()
        dequantize(1, 1, W2, HID)
        send(W2.at[HID:2 * HID, 0:HALF], W2.at[HID:2 * HID, HALF:WIDE], WTS + 1, WTS + 1, sib)
        got(A.at[other, :], ACTS + YLO, lo)
        acts_a[1].start()
        acts_b[0].start()
        loads[4].wait()
        down.wait()
        dequantize(0, 2, WD, 0)
        send(WD.at[:, 0:HALF], WD.at[:, HALF:WIDE], WTS + 2, WTS + 2, sib)

    pl.run_scoped(opening, pltpu.VMEM((2, HID, HALF), jnp.int32), pltpu.VMEM((3, HID, HALF // GROUP), F32),
                  pltpu.VMEM((3, HALF // GROUP, HID), F32))

    def gate_up(k):
        block = A[rows(k), :]
        for part in range(2):
            r = slice(part * HID, (part + 1) * HID)
            TO[k, r, :] = nt(W2[r, :], block).astype(BF16)
        send(TO.at[k, 0:2 * HID, :], TR.at[k, 0:2 * HID, :], TFGU + k, TFGU + k, hi)

    def grad_hidden(k):
        TO[k, 2 * HID:3 * HID, :] = nt(WD[...], C[rows(k), :]).astype(BF16)

    def send_grad_hidden(k):
        send(TO.at[k, 2 * HID:3 * HID, :], TR.at[k, 2 * HID:3 * HID, :], TFGH + k, TFGH + k, hi)

    def activate(k):
        got(TR.at[k, 0:2 * HID, :], TFGU + k, hi)
        sent(TO.at[k, 0:2 * HID, :], TFGU + k, hi)

        def tile(i, _):
            r, q = span(i * 32, 32), span(HID + i * 32, 32)
            gate = TO[k, r, :].astype(F32) + TR[k, r, :].astype(F32)
            up = TO[k, q, :].astype(F32) + TR[k, q, :].astype(F32)
            s = 1.0 / (1.0 + jnp.exp(-gate))
            silu = gate * s
            TO[k, r, :] = (silu * up).astype(BF16)
            TR[k, r, :] = silu.astype(BF16)
            TR[k, q, :] = (up * (s * (1.0 + gate * (1.0 - s)))).astype(BF16)
            return 0

        lax.fori_loop(0, HID // 32, tile, 0)

    def transpose(k):
        HT[...] = jnp.transpose(TO[k, 0:HID, :].astype(F32)).astype(BF16)

    def oslot(d, h):
        return span(((d - 1) * 2 + h) * CH, CH)

    def rslot(i):
        return span(i * CH, CH)

    def output_part(d, h):
        k = chunk(d, h)
        activate(k)
        transpose(k)
        o = oslot(d, h)

        def tile(i, _):
            cols = span(i * 512, 512)
            O[o, cols] = nn(HT[...], WD[:, cols]).astype(BF16)
            return 0

        lax.fori_loop(0, WIDE // 512, tile, 0)

    def loop(n, body):
        lax.fori_loop(0, n, lambda i, _: (body(i), 0)[1], 0)

    acts_a[1].forward()
    acts_b[1].start()
    acts_b[2].start()
    for part in range(2):
        got(W2.at[part * HID:(part + 1) * HID, HALF:WIDE], WTS + part, sib)
    gate_up(chunk(0, 0))
    acts_a[0].finish()
    acts_a[1].finish()
    acts_b[3].start()
    gate_up(chunk(0, 1))
    cot_a[0].forward()
    got(C.at[other, :], COT + YLO, lo)
    cot_a[1].start()
    acts_b[0].forward()
    acts_b[1].forward()
    loop(2, lambda j: gate_up(chunk(1 + 2 * j, 0)))
    cot_a[1].forward()
    acts_b[2].forward()
    acts_b[3].forward()
    cot_a[0].finish()
    cot_a[1].finish()
    for r in cot_b:
        r.start()
    loop(2, lambda j: gate_up(chunk(1 + 2 * j, 1)))
    loop(2, lambda h: activate(chunk(0, h)))
    acts_b[0].finish()
    acts_b[1].finish()
    gate_up(chunk(2, 0))
    acts_b[2].finish()
    acts_b[3].finish()
    gate_up(chunk(2, 1))

    for part in range(2):
        sent(W2.at[part * HID:(part + 1) * HID, 0:HALF], WTS + part, sib)
    pl.semaphore_signal(credit, inc=1, device_id=sib, device_id_type=MESH)

    got(WD.at[:, HALF:WIDE], WTS + 2, sib)
    output_part(1, 0)
    cot_b[0].forward()
    cot_b[1].forward()
    loop(2, lambda h: grad_hidden(chunk(0, h)))
    output_part(3, 0)
    send(O.at[oslot(3, 0), :], RB.at[rslot(4), :], RSB + 4, RSB + 4, bpeer(3))
    cot_b[2].forward()
    cot_b[3].forward()
    loop(2, lambda j: grad_hidden(chunk(1 + 2 * j, 0)))
    output_part(1, 1)
    send(O.at[oslot(1, 1), :], RB.at[rslot(3), :], RSB + 3, RSB + 3, bpeer(1))
    loop(2, lambda j: grad_hidden(chunk(1 + 2 * j, 1)))
    output_part(3, 1)
    output_part(2, 0)
    send(O.at[oslot(2, 0), :], RB.at[rslot(0), :], RSB, RSB, bpeer(1))
    loop(2, lambda h: send_grad_hidden(chunk(0, h)))
    output_part(2, 1)
    send(O.at[oslot(2, 1), :], RB.at[rslot(1), :], RSB + 1, RSB + 1, bpeer(3))
    loop(2, lambda j: send_grad_hidden(chunk(1 + 2 * j, 0)))
    loop(2, lambda j: send_grad_hidden(chunk(1 + 2 * j, 1)))
    cot_b[0].finish()
    cot_b[1].finish()
    grad_hidden(chunk(2, 0))
    send_grad_hidden(chunk(2, 0))
    cot_b[2].finish()
    cot_b[3].finish()
    grad_hidden(chunk(2, 1))
    send_grad_hidden(chunk(2, 1))

    def closing(gsum, dsum):
        def down_step(k, _):
            def tile(i):
                cols = span(i * 512, 512)
                dsum[:, cols] += nn(TO[k, 0:HID, :], C[rows(k), cols])

            loop(WIDE // 512, tile)
            return 0

        def slopes(k):
            got(TR.at[k, 2 * HID:3 * HID, :], TFGH + k, hi)

            def tile(i):
                r, q, w = span(i * 32, 32), span(HID + i * 32, 32), span(2 * HID + i * 32, 32)
                grad = TO[k, w, :].astype(F32) + TR[k, w, :].astype(F32)
                TR[k, r, :] = (grad * TR[k, r, :].astype(F32)).astype(BF16)
                TR[k, q, :] = (grad * TR[k, q, :].astype(F32)).astype(BF16)

            loop(HID // 32, tile)

        def weigh(k, low, high):
            def tile(i, _):
                cols = span(i * 256, 256)
                gsum[:, cols] += nn(TR[k, 0:2 * HID, :], A[rows(k), cols])
                return 0

            lax.fori_loop(low, high, tile, 0)

        def gate_step(k):
            slopes(k)
            weigh(k, 0, WIDE // 256)

        gsum[...] = jnp.zeros_like(gsum)
        dsum[...] = jnp.zeros_like(dsum)
        lax.fori_loop(0, 8, down_step, 0)

        def narrow(i):
            r = span(i * 32, 32)
            DS[r, :] = dsum[r, HALF:WIDE].astype(BF16)

        loop(HID // 32, narrow)
        send(DS, DR, GRD, GRD, sib)

        loop(2, lambda h: gate_step(chunk(0, h)))

        def add_share(buf, r, other_buf, q):
            def tile(i):
                cols = span(i * 512, 512)
                buf[r, cols] = (buf[r, cols].astype(F32) + other_buf[q, cols].astype(F32)).astype(BF16)

            loop(WIDE // 512, tile)

        got(RB.at[rslot(0), :], RSB, bpeer(3))
        add_share(O, oslot(1, 0), RB, rslot(0))
        send(O.at[oslot(1, 0), :], RB.at[rslot(2), :], RSB + 2, RSB + 2, bpeer(1))
        got(RB.at[rslot(1), :], RSB + 1, bpeer(1))
        add_share(O, oslot(3, 1), RB, rslot(1))
        send(O.at[oslot(3, 1), :], RB.at[rslot(5), :], RSB + 5, RSB + 5, bpeer(3))

        loop(2, lambda j: gate_step(chunk(1 + 2 * j, 0)))

        got(RB.at[rslot(3), :], RSB + 3, bpeer(3))
        got(RB.at[rslot(4), :], RSB + 4, bpeer(1))
        got(RB.at[rslot(2), :], RSB + 2, bpeer(3))
        got(RB.at[rslot(5), :], RSB + 5, bpeer(1))

        def badd(h):
            transpose(chunk(0, h))
            q, w = rslot(2 + h), rslot(4 + h)

            def tile(i):
                cols = span(i * 256, 256)
                total = nn(HT[...], WD[:, cols]) + RB[q, cols].astype(F32) + RB[w, cols].astype(F32)
                RB[q, cols] = total.astype(BF16)

            loop(WIDE // 256, tile)

        loop(2, badd)

        def part(d, y):
            a_ = (a + d) % 4
            return span(2 * CH + ((a_ // 2 + a // 2) % 2) * CH + (a_ % 2) * 2 * BLK + y * BLK, BLK)

        def slot(i):
            return span(i * BLK, BLK)

        send(RB.at[part(2, 0), :], RA.at[slot(0), :], RSA, RSA, apeer(1))
        send(RB.at[part(2, 1), :], RA.at[slot(1), :], RSA + 1, RSA + 1, apeer(3))
        send(RB.at[part(1, 1), :], RA.at[slot(3), :], RSA + 3, RSA + 3, apeer(1))
        send(RB.at[part(3, 0), :], RA.at[slot(4), :], RSA + 4, RSA + 4, apeer(3))
        gate_step(chunk(1, 1))
        got(RA.at[slot(0), :], RSA, apeer(3))
        add_share(RB, part(1, 0), RA, slot(0))
        send(RB.at[part(1, 0), :], RA.at[slot(2), :], RSA + 2, RSA + 2, apeer(1))
        got(RA.at[slot(1), :], RSA + 1, apeer(1))
        add_share(RB, part(3, 1), RA, slot(1))
        send(RB.at[part(3, 1), :], RA.at[slot(5), :], RSA + 5, RSA + 5, apeer(3))
        gate_step(chunk(3, 1))
        got(RA.at[slot(3), :], RSA + 3, apeer(3))
        got(RA.at[slot(4), :], RSA + 4, apeer(1))
        got(RA.at[slot(2), :], RSA + 2, apeer(3))
        got(RA.at[slot(5), :], RSA + 5, apeer(1))

        def aadd(y):
            def tile(i):
                cols = span(i * 512, 512)
                total = RB[part(0, y), cols].astype(F32) + RA[slot(2 + y), cols].astype(F32) + RA[slot(4 + y), cols].astype(F32)
                RB[part(0, y), cols] = total.astype(BF16)

            loop(WIDE // 512, tile)

        aadd(1 - ylo)
        send(RB.at[part(0, 1 - ylo), :], RY, RSY, RSY, lo)
        aadd(ylo)
        got(DR, GRD, sib)

        def down_add(i):
            r = span(i * 32, 32)
            dsum[r, 0:HALF] += DR[r, :].astype(F32)

        loop(HID // 32, down_add)
        put_down = local(dsum.at[:, 0:HALF], gd, 1)
        put_down.start()
        gate_step(chunk(2, 0))

        last = chunk(2, 1)
        slopes(last)
        weigh(last, HALF // 256, WIDE // 256)
        pl.semaphore_wait(credit, 1)

        def narrow_gates(i):
            r = span(i * 32, 32)
            W2[r, 0:HALF] = gsum[r, HALF:WIDE].astype(BF16)

        loop(2 * HID // 32, narrow_gates)
        send(W2.at[:, 0:HALF], W2.at[:, HALF:WIDE], GRU, GRU, sib)
        weigh(last, 0, HALF // 256)

        got(RY, RSY, lo)
        add_share(RB, part(0, ylo), RY, pl.ds(0, BLK))
        send(RB.at[part(0, ylo), HALF:WIDE], out.at[mine, :], OUTS, OUTS, sib)
        keep = local(RB.at[part(0, ylo), 0:HALF], out.at[mine, :], 0)
        keep.start()
        got(W2.at[:, HALF:WIDE], GRU, sib)

        def gates_add(i):
            r = span(i * 32, 32)
            gsum[r, 0:HALF] += W2[r, HALF:WIDE].astype(F32)

        loop(2 * HID // 32, gates_add)
        put_up = local(gsum.at[0:HID, 0:HALF], gu, 2)
        put_gate = local(gsum.at[HID:2 * HID, 0:HALF], gg, 3)
        put_up.start()
        put_gate.start()

        sent(acts.at[theirs, :], ACTS + SIB, sib)
        sent(cot.at[theirs, :], COT + SIB, sib)
        sent(A.at[own, :], ACTS + YLO, lo)
        sent(C.at[own, :], COT + YLO, lo)
        for r in acts_a + acts_b + cot_a + cot_b:
            r.drain()
        sent(WD.at[:, 0:HALF], WTS + 2, sib)
        for k in range(8):
            sent(TO.at[k, 2 * HID:3 * HID, :], TFGH + k, hi)
        for i in range(6):
            sent(O.at[rslot(i), :], RSB + i, bpeer(1))
            sent(RA.at[slot(i), :], RSA + i, apeer(1))
        sent(RY, RSY, lo)
        sent(RB.at[part(0, ylo), HALF:WIDE], OUTS, sib)
        sent(DS, GRD, sib)
        sent(W2.at[:, 0:HALF], GRU, sib)
        got(out.at[theirs, :], OUTS, sib)
        keep.wait()
        put_down.wait()
        put_up.wait()
        put_gate.wait()

    pl.run_scoped(closing, pltpu.VMEM((2 * HID, WIDE), F32), pltpu.VMEM((HID, WIDE), F32))


def hand_over(*refs):
    kept, results, held, sems = refs[0:4], refs[4:8], refs[8:12], refs[12]
    pieces = [(i, j) for i in (1, 2, 3, 0) for j in range(1 if i == 0 else 2)]
    way_in, way_out = [], []
    for n, (i, j) in enumerate(pieces):
        r = pl.ds(0, 2 * BLK) if i == 0 else pl.ds(j * HID // 2, HID // 2)
        way_in.append(pltpu.make_async_copy(kept[i].at[r, :], held[i].at[r, :], sems.at[n]))
        way_out.append(pltpu.make_async_copy(held[i].at[r, :], results[i].at[r, :], sems.at[len(pieces) + n]))
    for copy in way_in:
        copy.start()
    for before, after in zip(way_in, way_out):
        before.wait()
        after.start()
    for copy in way_out:
        copy.wait()


def local_step(acts, gc, gs, uc, us, dc, ds, cot):
    anywhere = pl.BlockSpec(memory_space=pl.ANY)
    results = pl.pallas_call(
        kernel,
        out_shape=(
            jax.ShapeDtypeStruct((2 * BLK, HALF), BF16),
            jax.ShapeDtypeStruct((HID, HALF), F32),
            jax.ShapeDtypeStruct((HID, HALF), F32),
            jax.ShapeDtypeStruct((HID, HALF), F32),
        ),
        in_specs=[anywhere] * 8,
        out_specs=(anywhere,) * 4,
        scratch_shapes=[
            pltpu.VMEM((8 * CH, WIDE), BF16),
            pltpu.VMEM((8 * CH, WIDE), BF16),
            pltpu.VMEM((2 * HID, WIDE), BF16),
            pltpu.VMEM((HID, WIDE), BF16),
            pltpu.VMEM((8, 3 * HID, CH), BF16),
            pltpu.VMEM((8, 3 * HID, CH), BF16),
            pltpu.VMEM((6 * CH, WIDE), BF16),
            pltpu.VMEM((6 * CH, WIDE), BF16),
            pltpu.VMEM((6 * BLK, WIDE), BF16),
            pltpu.VMEM((BLK, WIDE), BF16),
            pltpu.VMEM((CH, HID), BF16),
            pltpu.VMEM((HID, HALF), BF16),
            pltpu.VMEM((HID, HALF), BF16),
            pltpu.SemaphoreType.DMA((NSEM,)),
            pltpu.SemaphoreType.DMA((NSEM,)),
            pltpu.SemaphoreType.DMA((8,)),
            pltpu.SemaphoreType.REGULAR,
        ],
        compiler_params=pltpu.CompilerParams(collective_id=0, has_side_effects=True, vmem_limit_bytes=63 << 20),
        name="swiglu_step",
    )(acts, gc, gs.T, uc, us.T, dc, ds.T, cot)
    return pl.pallas_call(
        hand_over,
        out_shape=tuple(jax.ShapeDtypeStruct(r.shape, r.dtype) for r in results),
        in_specs=[anywhere] * 4,
        out_specs=(anywhere,) * 4,
        scratch_shapes=[pltpu.VMEM(r.shape, r.dtype) for r in results] + [pltpu.SemaphoreType.DMA((14,))],
        compiler_params=pltpu.CompilerParams(vmem_limit_bytes=60 << 20),
        name="hand_over",
    )(*results)


def solution(mesh):
    spec = P("fsdp", "tp")
    return jax.shard_map(local_step, mesh=mesh, in_specs=(spec,) * 8, out_specs=(spec,) * 4, check_vma=False)
```

time: 244 us -> 176 us (0.72)
  Pallas kernels: 227 us -> 172 us
  local copies, waits for them, and re-layouts: 12.8 us -> 0 us
    pallas_call x1, Pallas kernels: 227 us -> 167 us  [local_step(): pl.pallas_call(kernel, out_shape=(jax.ShapeDtypeStruct((2 * BLK, HALF), B...]
    unnamed x11 -> x0, local copies, waits for them, and re-layouts: 12.8 us -> none
    pallas_call x0 -> x1, Pallas kernels: none -> 4.83 us  [local_step(): pl.pallas_call(hand_over, out_shape=tuple((jax.ShapeDtypeStruct(r.shape,...]
where the time goes in v2:
time: 176 us; the launch traced here: 173 us
  Pallas kernels  172 us (98%)
    pallas_call x1, Pallas kernels, local_step(): pl.pallas_call(kernel, out_shape=(jax.ShapeDtypeStruct((2 * BLK, HALF), B...  167 us
    pallas_call x1, Pallas kernels, local_step(): pl.pallas_call(hand_over, out_shape=tuple((jax.ShapeDtypeStruct(r.shape,...  4.83 us

profile of v2, /device:TPU:0, one launch (start us, length us, event | category | flops | bytes accessed | tf_op | source)
XLA Modules:
  0.0 172.7 jit_solution(4911741378160286989)
XLA Ops:
  0.6 167.3 %swiglu_step.1 = (bf16[128,1024]{1,0:T(8,128)(2,1)}, f32[448,1024]{1,0:T(8,128)}, f32[448,1024]{1,0:T(8,128)}, f32[448,1024]{1,0:T(8,128)}) custom-call(bf16[128,1024]{1,0:T(8,128)(2,1)} %acts.1, s32[448,1024]{1,0:T(8,128)} %gc.1, f32[8,448]{1,0:T(8,128)} %bitcast.3, s32[448,1024]{1,0:T(8,128)} %uc.1, f32[8,448]{1,0:T(8,128)} %bitcast.4, s32[448,1024]{1,0:T(8,128)} %dc.1, ...), custom_call_target="tpu_custom_call" | custom-call | tf_op jit(solution)/shard_map/swiglu_step/pallas_call | solution.py:510
  167.9 4.8 %hand_over.1 = (bf16[128,1024]{1,0:T(8,128)(2,1)}, f32[448,1024]{1,0:T(8,128)}, f32[448,1024]{1,0:T(8,128)}, f32[448,1024]{1,0:T(8,128)}) custom-call(bf16[128,1024]{1,0:T(8,128)(2,1)} %get-tuple-element.8.refs_0_, f32[448,1024]{1,0:T(8,128)} %get-tuple-element.9.refs_1_, f32[448,1024]{1,0:T(8,128)} %get-tuple-element.10.refs_2_, ...), custom_call_target="tpu_custom_call" | custom-call | tf_op jit(solution)/shard_map/hand_over/pallas_call | solution.py:542

commit v3 on v2

--- a/solution.py
+++ b/solution.py
@@ -16,8 +16,8 @@
 BLK = 64
 CH = 256
 
-ACTS, COT, WTS, TFGU, TFGH, RSB, RSA, RSY, OUTS, GRD, GRU, NSEM = 0, 26, 52, 55, 63, 71, 77, 83, 84, 85, 86, 87
-SIB, YLO, AOWN, ALO, BPAIR = 0, 1, 2, 6, 10
+ACTS, COT, WTS, TFGU, TFGH, RSB, RSA, RSY, OUTS, GRD, GRU, PAIRS, NSEM = 0, 27, 54, 57, 65, 73, 79, 85, 86, 87, 88, 92, 94
+SIB, YLO, YSIB, AOWN, ALO, BPAIR = 0, 1, 2, 3, 7, 11
 
 
 def nt(left, right):
@@ -47,6 +47,7 @@
 
     sib = dev(x, ylo, z, yhi, 1 - c)
     lo = dev(x, 1 - ylo, z, yhi, c)
+    losib = dev(x, 1 - ylo, z, yhi, 1 - c)
     hi = dev(x, ylo, z, 1 - yhi, c)
 
     def rc(src, dst, s, r, to):
@@ -126,6 +127,10 @@
 
     acts_a, acts_b = rounds(A, ACTS)
     cot_a, cot_b = rounds(C, COT)
+
+    def got_other(buf, base):
+        got(buf.at[other, 0:HALF], base + YLO, lo)
+        got(buf.at[other, HALF:WIDE], base + YSIB, losib)
 
     def opening(codes, scales, turned):
         loads = [local(gc, codes.at[0], 0), local(gs, turned.at[0], 1), local(uc, codes.at[1], 2), local(us, turned.at[1], 3),
@@ -136,20 +141,20 @@
             load.start()
 
         barrier = pltpu.get_barrier_semaphore()
-        peers = [sib, lo, hi, apeer(1), apeer(3), bpeer(1), bpeer(3)]
+        peers = [sib, lo, losib, hi, apeer(1), apeer(3), bpeer(1), bpeer(3)]
         for peer in peers:
             pl.semaphore_signal(barrier, inc=1, device_id=peer, device_id_type=MESH)
         pl.semaphore_wait(barrier, len(peers))
 
-        send(acts.at[theirs, :], A.at[sibs, HALF:WIDE], ACTS + SIB, ACTS + SIB, sib)
-        send(cot.at[theirs, :], C.at[sibs, HALF:WIDE], COT + SIB, COT + SIB, sib)
+        for x_, buf, base in ((acts, A, ACTS), (cot, C, COT)):
+            send(x_.at[theirs, :], buf.at[sibs, HALF:WIDE], base + SIB, base + SIB, sib)
+            send(x_.at[mine, :], buf.at[own, 0:HALF], base + YLO, base + YLO, lo)
+            send(x_.at[theirs, :], buf.at[sibs, HALF:WIDE], base + YSIB, base + YSIB, losib)
         own_acts.wait()
         got(A.at[own, HALF:WIDE], ACTS + SIB, sib)
-        send(A.at[own, :], A.at[own, :], ACTS + YLO, ACTS + YLO, lo)
         acts_a[0].start()
         own_cot.wait()
         got(C.at[own, HALF:WIDE], COT + SIB, sib)
-        send(C.at[own, :], C.at[own, :], COT + YLO, COT + YLO, lo)
         cot_a[0].start()
 
         def dequantize(slot, which, w, first):
@@ -176,16 +181,16 @@
         loads[3].wait()
         dequantize(1, 1, W2, HID)
         send(W2.at[HID:2 * HID, 0:HALF], W2.at[HID:2 * HID, HALF:WIDE], WTS + 1, WTS + 1, sib)
-        got(A.at[other, :], ACTS + YLO, lo)
+        got_other(A, ACTS)
         acts_a[1].start()
         acts_b[0].start()
+        for part in range(2):
+            got(W2.at[part * HID:(part + 1) * HID, HALF:WIDE], WTS + part, sib)
+        gate_up_pair(0)
         loads[4].wait()
         down.wait()
         dequantize(0, 2, WD, 0)
         send(WD.at[:, 0:HALF], WD.at[:, HALF:WIDE], WTS + 2, WTS + 2, sib)
-
-    pl.run_scoped(opening, pltpu.VMEM((2, HID, HALF), jnp.int32), pltpu.VMEM((3, HID, HALF // GROUP), F32),
-                  pltpu.VMEM((3, HALF // GROUP, HID), F32))
 
     def gate_up(k):
         block = A[rows(k), :]
@@ -194,15 +199,38 @@
             TO[k, r, :] = nt(W2[r, :], block).astype(BF16)
         send(TO.at[k, 0:2 * HID, :], TR.at[k, 0:2 * HID, :], TFGU + k, TFGU + k, hi)
 
+    def pair_cols(i):
+        return span(((order[i] % 2) * 2 * BLK), 2 * BLK)
+
+    def gate_up_pair(i):
+        k, cols = chunk(0, 0), pair_cols(i)
+        block = A[span((b * 4 + order[i]) * 2 * BLK, 2 * BLK), :]
+        for part in range(2):
+            r = slice(part * HID, (part + 1) * HID)
+            TO[k, r, cols] = nt(W2[r, :], block).astype(BF16)
+        send(TO.at[k, 0:2 * HID, cols], TR.at[k, 0:2 * HID, cols], PAIRS + i, PAIRS + i, hi)
+
+    pl.run_scoped(opening, pltpu.VMEM((2, HID, HALF), jnp.int32), pltpu.VMEM((3, HID, HALF // GROUP), F32),
+                  pltpu.VMEM((3, HALF // GROUP, HID), F32))
+
     def grad_hidden(k):
         TO[k, 2 * HID:3 * HID, :] = nt(WD[...], C[rows(k), :]).astype(BF16)
 
     def send_grad_hidden(k):
         send(TO.at[k, 2 * HID:3 * HID, :], TR.at[k, 2 * HID:3 * HID, :], TFGH + k, TFGH + k, hi)
 
-    def activate(k):
-        got(TR.at[k, 0:2 * HID, :], TFGU + k, hi)
-        sent(TO.at[k, 0:2 * HID, :], TFGU + k, hi)
+    def hidden_share(k):
+        grad_hidden(k)
+        send_grad_hidden(k)
+
+    def activate(k, pairs=False):
+        if pairs:
+            for i in range(2):
+                got(TR.at[k, 0:2 * HID, pair_cols(i)], PAIRS + i, hi)
+                sent(TO.at[k, 0:2 * HID, pair_cols(i)], PAIRS + i, hi)
+        else:
+            got(TR.at[k, 0:2 * HID, :], TFGU + k, hi)
+            sent(TO.at[k, 0:2 * HID, :], TFGU + k, hi)
 
         def tile(i, _):
             r, q = span(i * 32, 32), span(HID + i * 32, 32)
@@ -242,80 +270,13 @@
     def loop(n, body):
         lax.fori_loop(0, n, lambda i, _: (body(i), 0)[1], 0)
 
-    acts_a[1].forward()
-    acts_b[1].start()
-    acts_b[2].start()
-    for part in range(2):
-        got(W2.at[part * HID:(part + 1) * HID, HALF:WIDE], WTS + part, sib)
-    gate_up(chunk(0, 0))
-    acts_a[0].finish()
-    acts_a[1].finish()
-    acts_b[3].start()
-    gate_up(chunk(0, 1))
-    cot_a[0].forward()
-    got(C.at[other, :], COT + YLO, lo)
-    cot_a[1].start()
-    acts_b[0].forward()
-    acts_b[1].forward()
-    loop(2, lambda j: gate_up(chunk(1 + 2 * j, 0)))
-    cot_a[1].forward()
-    acts_b[2].forward()
-    acts_b[3].forward()
-    cot_a[0].finish()
-    cot_a[1].finish()
-    for r in cot_b:
-        r.start()
-    loop(2, lambda j: gate_up(chunk(1 + 2 * j, 1)))
-    loop(2, lambda h: activate(chunk(0, h)))
-    acts_b[0].finish()
-    acts_b[1].finish()
-    gate_up(chunk(2, 0))
-    acts_b[2].finish()
-    acts_b[3].finish()
-    gate_up(chunk(2, 1))
-
-    for part in range(2):
-        sent(W2.at[part * HID:(part + 1) * HID, 0:HALF], WTS + part, sib)
-    pl.semaphore_signal(credit, inc=1, device_id=sib, device_id_type=MESH)
-
-    got(WD.at[:, HALF:WIDE], WTS + 2, sib)
-    output_part(1, 0)
-    cot_b[0].forward()
-    cot_b[1].forward()
-    loop(2, lambda h: grad_hidden(chunk(0, h)))
-    output_part(3, 0)
-    send(O.at[oslot(3, 0), :], RB.at[rslot(4), :], RSB + 4, RSB + 4, bpeer(3))
-    cot_b[2].forward()
-    cot_b[3].forward()
-    loop(2, lambda j: grad_hidden(chunk(1 + 2 * j, 0)))
-    output_part(1, 1)
-    send(O.at[oslot(1, 1), :], RB.at[rslot(3), :], RSB + 3, RSB + 3, bpeer(1))
-    loop(2, lambda j: grad_hidden(chunk(1 + 2 * j, 1)))
-    output_part(3, 1)
-    output_part(2, 0)
-    send(O.at[oslot(2, 0), :], RB.at[rslot(0), :], RSB, RSB, bpeer(1))
-    loop(2, lambda h: send_grad_hidden(chunk(0, h)))
-    output_part(2, 1)
-    send(O.at[oslot(2, 1), :], RB.at[rslot(1), :], RSB + 1, RSB + 1, bpeer(3))
-    loop(2, lambda j: send_grad_hidden(chunk(1 + 2 * j, 0)))
-    loop(2, lambda j: send_grad_hidden(chunk(1 + 2 * j, 1)))
-    cot_b[0].finish()
-    cot_b[1].finish()
-    grad_hidden(chunk(2, 0))
-    send_grad_hidden(chunk(2, 0))
-    cot_b[2].finish()
-    cot_b[3].finish()
-    grad_hidden(chunk(2, 1))
-    send_grad_hidden(chunk(2, 1))
-
-    def closing(gsum, dsum):
-        def down_step(k, _):
+    def middle(gsum, dsum):
+        def down_step(k):
             def tile(i):
                 cols = span(i * 512, 512)
                 dsum[:, cols] += nn(TO[k, 0:HID, :], C[rows(k), cols])
 
             loop(WIDE // 512, tile)
-            return 0
 
         def slopes(k):
             got(TR.at[k, 2 * HID:3 * HID, :], TFGH + k, hi)
@@ -328,30 +289,12 @@
 
             loop(HID // 32, tile)
 
-        def weigh(k, low, high):
-            def tile(i, _):
-                cols = span(i * 256, 256)
-                gsum[:, cols] += nn(TR[k, 0:2 * HID, :], A[rows(k), cols])
-                return 0
-
-            lax.fori_loop(low, high, tile, 0)
+        def weigh(k, cols):
+            gsum[:, cols] += nn(TR[k, 0:2 * HID, :], A[rows(k), cols])
 
         def gate_step(k):
             slopes(k)
-            weigh(k, 0, WIDE // 256)
-
-        gsum[...] = jnp.zeros_like(gsum)
-        dsum[...] = jnp.zeros_like(dsum)
-        lax.fori_loop(0, 8, down_step, 0)
-
-        def narrow(i):
-            r = span(i * 32, 32)
-            DS[r, :] = dsum[r, HALF:WIDE].astype(BF16)
-
-        loop(HID // 32, narrow)
-        send(DS, DR, GRD, GRD, sib)
-
-        loop(2, lambda h: gate_step(chunk(0, h)))
+            loop(WIDE // 256, lambda i: weigh(k, span(i * 256, 256)))
 
         def add_share(buf, r, other_buf, q):
             def tile(i):
@@ -360,32 +303,138 @@
 
             loop(WIDE // 512, tile)
 
+        acts_a[1].forward()
+        acts_b[1].start()
+        acts_b[2].start()
+        gate_up_pair(1)
+        acts_a[0].finish()
+        acts_a[1].finish()
+        acts_b[3].start()
+        gate_up(chunk(0, 1))
+        cot_a[0].forward()
+        got_other(C, COT)
+        cot_a[1].start()
+        acts_b[0].forward()
+        acts_b[1].forward()
+        loop(2, lambda j: gate_up(chunk(1 + 2 * j, 0)))
+        cot_a[1].forward()
+        acts_b[2].forward()
+        acts_b[3].forward()
+        cot_a[0].finish()
+        cot_a[1].finish()
+        cot_b[0].start()
+        cot_b[1].start()
+        cot_b[2].start()
+        cot_b[3].start()
+
+        def clear(i):
+            gsum[span(i * 32, 32), :] = jnp.zeros((32, WIDE), F32)
+
+        loop(2 * HID // 32, clear)
+
+        def clear_down(i):
+            dsum[span(i * 32, 32), :] = jnp.zeros((32, WIDE), F32)
+
+        loop(HID // 32, clear_down)
+        got(WD.at[:, HALF:WIDE], WTS + 2, sib)
+        loop(2, lambda h: grad_hidden(chunk(0, h)))
+        acts_b[0].finish()
+        acts_b[1].finish()
+        gate_up(chunk(2, 0))
+        acts_b[2].finish()
+        acts_b[3].finish()
+        gate_up(chunk(2, 1))
+        loop(2, lambda j: gate_up(chunk(1 + 2 * j, 1)))
+        loop(2, lambda h: send_grad_hidden(chunk(0, h)))
+
+        for part in range(2):
+            sent(W2.at[part * HID:(part + 1) * HID, 0:HALF], WTS + part, sib)
+        pl.semaphore_signal(credit, inc=1, device_id=sib, device_id_type=MESH)
+
+        def share(d, h, s, i):
+            send(O.at[oslot(d, h), :], RB.at[rslot(i), :], RSB + i, RSB + i, bpeer(s))
+
+        activate(chunk(0, 0), True)
+        down_step(chunk(0, 0))
+        output_part(1, 0)
+        output_part(3, 0)
+        share(3, 0, 3, 4)
+        activate(chunk(0, 1))
+        down_step(chunk(0, 1))
+        cot_b[0].forward()
+        cot_b[1].forward()
+        loop(2, lambda j: hidden_share(chunk(1 + 2 * j, 0)))
+        output_part(2, 0)
+        share(2, 0, 1, 0)
+        loop(2, lambda j: down_step(chunk(1 + 2 * j, 0)))
+        cot_b[2].forward()
+        output_part(2, 1)
+        share(2, 1, 3, 1)
+        cot_b[3].forward()
+        loop(2, lambda j: hidden_share(chunk(1 + 2 * j, 1)))
+        output_part(1, 1)
+        share(1, 1, 1, 3)
+        down_step(chunk(1, 1))
+        cot_b[0].finish()
+        cot_b[1].finish()
+        hidden_share(chunk(2, 0))
+        down_step(chunk(2, 0))
         got(RB.at[rslot(0), :], RSB, bpeer(3))
         add_share(O, oslot(1, 0), RB, rslot(0))
-        send(O.at[oslot(1, 0), :], RB.at[rslot(2), :], RSB + 2, RSB + 2, bpeer(1))
+        share(1, 0, 1, 2)
+        output_part(3, 1)
         got(RB.at[rslot(1), :], RSB + 1, bpeer(1))
         add_share(O, oslot(3, 1), RB, rslot(1))
-        send(O.at[oslot(3, 1), :], RB.at[rslot(5), :], RSB + 5, RSB + 5, bpeer(3))
-
+        share(3, 1, 3, 5)
+        down_step(chunk(3, 1))
+        cot_b[2].finish()
+        cot_b[3].finish()
+        hidden_share(chunk(2, 1))
+        down_step(chunk(2, 1))
+
+        def narrow(i):
+            r = span(i * 32, 32)
+            DS[r, :] = dsum[r, HALF:WIDE].astype(BF16)
+
+        loop(HID // 32, narrow)
+        send(DS, DR, GRD, GRD, sib)
+        gate_step(chunk(0, 0))
+
+        sent(O.at[oslot(2, 0), :], RSB, bpeer(1))
+        sent(O.at[oslot(2, 1), :], RSB + 1, bpeer(3))
+
+        def own_part(h):
+            transpose(chunk(0, h))
+            o = oslot(2, h)
+
+            def tile(i):
+                cols = span(i * 512, 512)
+                O[o, cols] = nn(HT[...], WD[:, cols]).astype(BF16)
+
+            loop(WIDE // 512, tile)
+
+        loop(2, own_part)
+        gate_step(chunk(0, 1))
+        got(DR, GRD, sib)
+
+        def down_add(i):
+            r = span(i * 32, 32)
+            dsum[r, 0:HALF] += DR[r, :].astype(F32)
+
+        loop(HID // 32, down_add)
+        put_down = local(dsum.at[:, 0:HALF], gd, 1)
+        put_down.start()
         loop(2, lambda j: gate_step(chunk(1 + 2 * j, 0)))
 
-        got(RB.at[rslot(3), :], RSB + 3, bpeer(3))
-        got(RB.at[rslot(4), :], RSB + 4, bpeer(1))
-        got(RB.at[rslot(2), :], RSB + 2, bpeer(3))
-        got(RB.at[rslot(5), :], RSB + 5, bpeer(1))
-
         def badd(h):
-            transpose(chunk(0, h))
-            q, w = rslot(2 + h), rslot(4 + h)
+            o, q, w = oslot(2, h), rslot(2 + h), rslot(4 + h)
 
             def tile(i):
                 cols = span(i * 256, 256)
-                total = nn(HT[...], WD[:, cols]) + RB[q, cols].astype(F32) + RB[w, cols].astype(F32)
+                total = O[o, cols].astype(F32) + RB[q, cols].astype(F32) + RB[w, cols].astype(F32)
                 RB[q, cols] = total.astype(BF16)
 
             loop(WIDE // 256, tile)
-
-        loop(2, badd)
 
         def part(d, y):
             a_ = (a + d) % 4
@@ -394,18 +443,24 @@
         def slot(i):
             return span(i * BLK, BLK)
 
+        got(RB.at[rslot(3), :], RSB + 3, bpeer(3))
+        got(RB.at[rslot(5), :], RSB + 5, bpeer(1))
+        badd(1)
         send(RB.at[part(2, 0), :], RA.at[slot(0), :], RSA, RSA, apeer(1))
         send(RB.at[part(2, 1), :], RA.at[slot(1), :], RSA + 1, RSA + 1, apeer(3))
+        got(RB.at[rslot(4), :], RSB + 4, bpeer(1))
+        got(RB.at[rslot(2), :], RSB + 2, bpeer(3))
+        badd(0)
         send(RB.at[part(1, 1), :], RA.at[slot(3), :], RSA + 3, RSA + 3, apeer(1))
         send(RB.at[part(3, 0), :], RA.at[slot(4), :], RSA + 4, RSA + 4, apeer(3))
-        gate_step(chunk(1, 1))
+        gate_step(chunk(2, 0))
         got(RA.at[slot(0), :], RSA, apeer(3))
         add_share(RB, part(1, 0), RA, slot(0))
         send(RB.at[part(1, 0), :], RA.at[slot(2), :], RSA + 2, RSA + 2, apeer(1))
         got(RA.at[slot(1), :], RSA + 1, apeer(1))
         add_share(RB, part(3, 1), RA, slot(1))
         send(RB.at[part(3, 1), :], RA.at[slot(5), :], RSA + 5, RSA + 5, apeer(3))
-        gate_step(chunk(3, 1))
+        gate_step(chunk(1, 1))
         got(RA.at[slot(3), :], RSA + 3, apeer(3))
         got(RA.at[slot(4), :], RSA + 4, apeer(1))
         got(RA.at[slot(2), :], RSA + 2, apeer(3))
@@ -422,70 +477,70 @@
         aadd(1 - ylo)
         send(RB.at[part(0, 1 - ylo), :], RY, RSY, RSY, lo)
         aadd(ylo)
-        got(DR, GRD, sib)
-
-        def down_add(i):
-            r = span(i * 32, 32)
-            dsum[r, 0:HALF] += DR[r, :].astype(F32)
-
-        loop(HID // 32, down_add)
-        put_down = local(dsum.at[:, 0:HALF], gd, 1)
-        put_down.start()
-        gate_step(chunk(2, 0))
+        gate_step(chunk(3, 1))
 
         last = chunk(2, 1)
         slopes(last)
-        weigh(last, HALF // 256, WIDE // 256)
         pl.semaphore_wait(credit, 1)
 
-        def narrow_gates(i):
-            r = span(i * 32, 32)
-            W2[r, 0:HALF] = gsum[r, HALF:WIDE].astype(BF16)
-
-        loop(2 * HID // 32, narrow_gates)
-        send(W2.at[:, 0:HALF], W2.at[:, HALF:WIDE], GRU, GRU, sib)
-        weigh(last, 0, HALF // 256)
+        def piece(i):
+            return span(i * 256, 256)
+
+        def far_piece(i):
+            return span(HALF + i * 256, 256)
+
+        def give(i):
+            weigh(last, far_piece(i))
+            W2[:, piece(i)] = gsum[:, far_piece(i)].astype(BF16)
+            send(W2.at[:, piece(i)], W2.at[:, far_piece(i)], GRU + i, GRU + i, sib)
+
+        loop(4, give)
+        loop(4, lambda i: weigh(last, piece(i)))
 
         got(RY, RSY, lo)
         add_share(RB, part(0, ylo), RY, pl.ds(0, BLK))
         send(RB.at[part(0, ylo), HALF:WIDE], out.at[mine, :], OUTS, OUTS, sib)
         keep = local(RB.at[part(0, ylo), 0:HALF], out.at[mine, :], 0)
         keep.start()
-        got(W2.at[:, HALF:WIDE], GRU, sib)
-
-        def gates_add(i):
-            r = span(i * 32, 32)
-            gsum[r, 0:HALF] += W2[r, HALF:WIDE].astype(F32)
-
-        loop(2 * HID // 32, gates_add)
-        put_up = local(gsum.at[0:HID, 0:HALF], gu, 2)
-        put_gate = local(gsum.at[HID:2 * HID, 0:HALF], gg, 3)
-        put_up.start()
-        put_gate.start()
-
-        sent(acts.at[theirs, :], ACTS + SIB, sib)
-        sent(cot.at[theirs, :], COT + SIB, sib)
-        sent(A.at[own, :], ACTS + YLO, lo)
-        sent(C.at[own, :], COT + YLO, lo)
+
+        def put(i):
+            up = local(gsum.at[0:HID, piece(i)], gu.at[:, piece(i)], 2 + 2 * i)
+            gate = local(gsum.at[HID:2 * HID, piece(i)], gg.at[:, piece(i)], 3 + 2 * i)
+            return up, gate
+
+        def take(i):
+            got(W2.at[:, far_piece(i)], GRU + i, sib)
+            gsum[:, piece(i)] += W2[:, far_piece(i)].astype(F32)
+            for copy in put(i):
+                copy.start()
+
+        loop(4, take)
+
+        for x_, buf, base in ((acts, A, ACTS), (cot, C, COT)):
+            sent(x_.at[theirs, :], base + SIB, sib)
+            sent(x_.at[mine, :], base + YLO, lo)
+            sent(x_.at[theirs, :], base + YSIB, losib)
         for r in acts_a + acts_b + cot_a + cot_b:
             r.drain()
         sent(WD.at[:, 0:HALF], WTS + 2, sib)
         for k in range(8):
             sent(TO.at[k, 2 * HID:3 * HID, :], TFGH + k, hi)
         for i in range(6):
+            sent(RA.at[slot(i), :], RSA + i, apeer(1))
+        for i in range(2, 6):
             sent(O.at[rslot(i), :], RSB + i, bpeer(1))
-            sent(RA.at[slot(i), :], RSA + i, apeer(1))
         sent(RY, RSY, lo)
         sent(RB.at[part(0, ylo), HALF:WIDE], OUTS, sib)
         sent(DS, GRD, sib)
-        sent(W2.at[:, 0:HALF], GRU, sib)
         got(out.at[theirs, :], OUTS, sib)
         keep.wait()
         put_down.wait()
-        put_up.wait()
-        put_gate.wait()
-
-    pl.run_scoped(closing, pltpu.VMEM((2 * HID, WIDE), F32), pltpu.VMEM((HID, WIDE), F32))
+        for i in range(4):
+            sent(W2.at[:, i * 256:(i + 1) * 256], GRU + i, sib)
+            for copy in put(i):
+                copy.wait()
+
+    pl.run_scoped(middle, pltpu.VMEM((2 * HID, WIDE), F32), pltpu.VMEM((HID, WIDE), F32))
 
 
 def hand_over(*refs):
@@ -533,7 +588,7 @@
             pltpu.VMEM((HID, HALF), BF16),
             pltpu.SemaphoreType.DMA((NSEM,)),
             pltpu.SemaphoreType.DMA((NSEM,)),
-            pltpu.SemaphoreType.DMA((8,)),
+            pltpu.SemaphoreType.DMA((10,)),
             pltpu.SemaphoreType.REGULAR,
         ],
         compiler_params=pltpu.CompilerParams(collective_id=0, has_side_effects=True, vmem_limit_bytes=63 << 20),

time: 176 us -> 162 us (0.920)
  Pallas kernels: 172 us -> 160 us
    pallas_call x1, Pallas kernels: 167 us -> 155 us  [local_step(): pl.pallas_call(kernel, out_shape=(jax.ShapeDtypeStruct((2 * BLK, HALF), B...]
where the time goes in v3:
time: 162 us; the launch traced here: 160 us
  Pallas kernels  160 us (99%)
    pallas_call x1, Pallas kernels, local_step(): pl.pallas_call(kernel, out_shape=(jax.ShapeDtypeStruct((2 * BLK, HALF), B...  155 us
    pallas_call x1, Pallas kernels, local_step(): pl.pallas_call(hand_over, out_shape=tuple((jax.ShapeDtypeStruct(r.shape,...  4.83 us

profile of v3, /device:TPU:0, one launch (start us, length us, event | category | flops | bytes accessed | tf_op | source)
XLA Modules:
  0.0 160.5 jit_solution(6079592845185178884)
XLA Ops:
  0.6 154.9 %swiglu_step.1 = (bf16[128,1024]{1,0:T(8,128)(2,1)}, f32[448,1024]{1,0:T(8,128)}, f32[448,1024]{1,0:T(8,128)}, f32[448,1024]{1,0:T(8,128)}) custom-call(bf16[128,1024]{1,0:T(8,128)(2,1)} %acts.1, s32[448,1024]{1,0:T(8,128)} %gc.1, f32[8,448]{1,0:T(8,128)} %bitcast.3, s32[448,1024]{1,0:T(8,128)} %uc.1, f32[8,448]{1,0:T(8,128)} %bitcast.4, s32[448,1024]{1,0:T(8,128)} %dc.1, ...), custom_call_target="tpu_custom_call" | custom-call | tf_op jit(solution)/shard_map/swiglu_step/pallas_call | solution.py:565
  155.5 4.8 %hand_over.1 = (bf16[128,1024]{1,0:T(8,128)(2,1)}, f32[448,1024]{1,0:T(8,128)}, f32[448,1024]{1,0:T(8,128)}, f32[448,1024]{1,0:T(8,128)}) custom-call(bf16[128,1024]{1,0:T(8,128)(2,1)} %get-tuple-element.8.refs_0_, f32[448,1024]{1,0:T(8,128)} %get-tuple-element.9.refs_1_, f32[448,1024]{1,0:T(8,128)} %get-tuple-element.10.refs_2_, ...), custom_call_target="tpu_custom_call" | custom-call | tf_op jit(solution)/shard_map/hand_over/pallas_call | solution.py:597

commit v4 on v3

--- a/solution.py
+++ b/solution.py
@@ -453,14 +453,14 @@
         badd(0)
         send(RB.at[part(1, 1), :], RA.at[slot(3), :], RSA + 3, RSA + 3, apeer(1))
         send(RB.at[part(3, 0), :], RA.at[slot(4), :], RSA + 4, RSA + 4, apeer(3))
-        gate_step(chunk(2, 0))
+        gate_step(chunk(1, 1))
         got(RA.at[slot(0), :], RSA, apeer(3))
         add_share(RB, part(1, 0), RA, slot(0))
         send(RB.at[part(1, 0), :], RA.at[slot(2), :], RSA + 2, RSA + 2, apeer(1))
         got(RA.at[slot(1), :], RSA + 1, apeer(1))
         add_share(RB, part(3, 1), RA, slot(1))
         send(RB.at[part(3, 1), :], RA.at[slot(5), :], RSA + 5, RSA + 5, apeer(3))
-        gate_step(chunk(1, 1))
+        gate_step(chunk(3, 1))
         got(RA.at[slot(3), :], RSA + 3, apeer(3))
         got(RA.at[slot(4), :], RSA + 4, apeer(1))
         got(RA.at[slot(2), :], RSA + 2, apeer(3))
@@ -477,7 +477,7 @@
         aadd(1 - ylo)
         send(RB.at[part(0, 1 - ylo), :], RY, RSY, RSY, lo)
         aadd(ylo)
-        gate_step(chunk(3, 1))
+        gate_step(chunk(2, 0))
 
         last = chunk(2, 1)
         slopes(last)
@@ -496,25 +496,25 @@
 
         loop(4, give)
         loop(4, lambda i: weigh(last, piece(i)))
+
+        def put(i):
+            up = local(gsum.at[0:HID, piece(i)], gu.at[:, piece(i)], 2 + 2 * i)
+            gate = local(gsum.at[HID:2 * HID, piece(i)], gg.at[:, piece(i)], 3 + 2 * i)
+            return up, gate
+
+        def take(i):
+            got(W2.at[:, far_piece(i)], GRU + i, sib)
+            gsum[:, piece(i)] += W2[:, far_piece(i)].astype(F32)
+            for copy in put(i):
+                copy.start()
+
+        loop(4, take)
 
         got(RY, RSY, lo)
         add_share(RB, part(0, ylo), RY, pl.ds(0, BLK))
         send(RB.at[part(0, ylo), HALF:WIDE], out.at[mine, :], OUTS, OUTS, sib)
         keep = local(RB.at[part(0, ylo), 0:HALF], out.at[mine, :], 0)
         keep.start()
-
-        def put(i):
-            up = local(gsum.at[0:HID, piece(i)], gu.at[:, piece(i)], 2 + 2 * i)
-            gate = local(gsum.at[HID:2 * HID, piece(i)], gg.at[:, piece(i)], 3 + 2 * i)
-            return up, gate
-
-        def take(i):
-            got(W2.at[:, far_piece(i)], GRU + i, sib)
-            gsum[:, piece(i)] += W2[:, far_piece(i)].astype(F32)
-            for copy in put(i):
-                copy.start()
-
-        loop(4, take)
 
         for x_, buf, base in ((acts, A, ACTS), (cot, C, COT)):
             sent(x_.at[theirs, :], base + SIB, sib)

time: 162 us -> 161 us (level)
  no operation moved by 1% of the time
where the time goes in v4:
time: 161 us; the launch traced here: 159 us
  Pallas kernels  159 us (99%)
    pallas_call x1, Pallas kernels, local_step(): pl.pallas_call(kernel, out_shape=(jax.ShapeDtypeStruct((2 * BLK, HALF), B...  154 us
    pallas_call x1, Pallas kernels, local_step(): pl.pallas_call(hand_over, out_shape=tuple((jax.ShapeDtypeStruct(r.shape,...  4.83 us

profile of v4, /device:TPU:0, one launch (start us, length us, event | category | flops | bytes accessed | tf_op | source)
XLA Modules:
  0.0 159.4 jit_solution(56515088685926046)
XLA Ops:
  0.6 153.8 %swiglu_step.1 = (bf16[128,1024]{1,0:T(8,128)(2,1)}, f32[448,1024]{1,0:T(8,128)}, f32[448,1024]{1,0:T(8,128)}, f32[448,1024]{1,0:T(8,128)}) custom-call(bf16[128,1024]{1,0:T(8,128)(2,1)} %acts.1, s32[448,1024]{1,0:T(8,128)} %gc.1, f32[8,448]{1,0:T(8,128)} %bitcast.3, s32[448,1024]{1,0:T(8,128)} %uc.1, f32[8,448]{1,0:T(8,128)} %bitcast.4, s32[448,1024]{1,0:T(8,128)} %dc.1, ...), custom_call_target="tpu_custom_call" | custom-call | tf_op jit(solution)/shard_map/swiglu_step/pallas_call | solution.py:565
  154.4 4.8 %hand_over.1 = (bf16[128,1024]{1,0:T(8,128)(2,1)}, f32[448,1024]{1,0:T(8,128)}, f32[448,1024]{1,0:T(8,128)}, f32[448,1024]{1,0:T(8,128)}) custom-call(bf16[128,1024]{1,0:T(8,128)(2,1)} %get-tuple-element.8.refs_0_, f32[448,1024]{1,0:T(8,128)} %get-tuple-element.9.refs_1_, f32[448,1024]{1,0:T(8,128)} %get-tuple-element.10.refs_2_, ...), custom_call_target="tpu_custom_call" | custom-call | tf_op jit(solution)/shard_map/hand_over/pallas_call | solution.py:597
